TPU v7x, 32 devices: a whole 2x2x4 slice. The times are simulated.
32 devices in a mesh: wave: 16 (over z, x, core), lev: 2 (over y).
Axes of the slice: x: 2, y: 2, z: 4, core: 2. Of those that a mesh axis runs over, the one named last changes fastest.
Arguments:
- control: bfloat16 [1536, 1536, 2, 137], P(('wave', 'lev')), may hold values from -6 to 6
- covariance: bfloat16 [1536, 64, 137], P(('wave', 'lev')), may hold values from -0.013671875 to 0.013671875
- legendre: bfloat16 [1536, 1536, 16], P(('wave', 'lev')), may hold values from -0.21875 to 0.21875
- wave_order: int32 [1536], replicated, may hold values from 0 to 1535, each once
- lat_order: int32 [32], replicated, may hold values from 0 to 31, each once
- cycle_points: int32 [16], replicated, may hold values from 2048 to 6160, as said below
Outputs:
- grid: bfloat16 [32, 64, 2048], P(('wave', 'lev'))
Inputs may be any that keep to these rules, and one draw needn't show every extreme that they name: cycle_points[i] is a multiple of 4, and at least 2048.
All inputs are finite; a program needn't handle non-finite values.
Results may differ from a plain program's by a relative error of at most 0.0062.
Values may be sent and summed in bfloat16 or wider, within the bound.
A program may use at most 192 MiB of HBM per device.

v0:
```python
import jax
import jax.numpy as jnp
from jax import lax
from jax.sharding import PartitionSpec as P

LONW = 2048


def trig_tables(orders, points, factor, width):
    coarse = jnp.arange(width // 64, dtype=jnp.int32) * 64
    fine = jnp.arange(64, dtype=jnp.int32)
    scale = 2.0 * jnp.pi / points.astype(jnp.float32)
    coarse_angle = (orders[:, None] * coarse[None, :] % points).astype(jnp.float32) * scale
    fine_angle = (orders[:, None] * fine[None, :] % points).astype(jnp.float32) * scale
    cos_c = jnp.cos(coarse_angle)[:, :, None]
    sin_c = jnp.sin(coarse_angle)[:, :, None]
    cos_f = jnp.cos(fine_angle)[:, None, :]
    sin_f = jnp.sin(fine_angle)[:, None, :]
    cosine = (cos_c * cos_f - sin_c * sin_f).reshape(orders.shape[0], width)
    sine = (sin_c * cos_f + cos_c * sin_f).reshape(orders.shape[0], width)
    cos_part = (factor[:, None] * cosine).astype(jnp.bfloat16)
    sin_part = (-factor[:, None] * sine).astype(jnp.bfloat16)
    return (cos_part, sin_part)


def shards(control, covariance, legendre, wave_order, lat_order, cycle_points):
    wave_count = lax.axis_size("wave")
    level_count = lax.axis_size("lev")
    own_totals = control.shape[0]
    total = control.shape[1]
    own_rows = legendre.shape[0]
    half_lats = legendre.shape[2]
    all_lats = lat_order.shape[0]
    own_lats = all_lats // (wave_count * level_count)
    flat_index = lax.axis_index(("wave", "lev"))
    total_ids = flat_index * own_totals + jnp.arange(own_totals, dtype=jnp.int32)
    usable = total_ids[:, None] >= wave_order[None, :]
    imag_usable = usable & (wave_order > 0)[None, :]
    weights = jnp.stack([usable, imag_usable], axis=2).astype(jnp.float32)
    produced = jnp.einsum("nrcl,nsl->nrcs", control, covariance, preferred_element_type=jnp.float32)
    slab = (produced * weights[:, :, :, None]).astype(jnp.bfloat16)
    slab_levels = slab.shape[3]
    moved = lax.all_to_all(
        lax.all_to_all(slab, "wave", split_axis=1, concat_axis=0, tiled=True),
        "lev",
        split_axis=1,
        concat_axis=0,
        tiled=True,
    )
    moved = moved.reshape(level_count, wave_count, own_totals, own_rows, 2, slab_levels)
    moved = jnp.transpose(moved, (1, 0, 2, 3, 4, 5)).reshape(total, own_rows, 2, slab_levels)
    own_orders = lax.dynamic_slice_in_dim(wave_order, flat_index * own_rows, own_rows, 0)
    odd_order = own_orders % 2 == 1
    paired = moved.reshape(total // 2, 2, own_rows, 2, slab_levels)
    pick_moved = odd_order[None, :, None, None]
    even_moved = jnp.where(pick_moved, paired[:, 1], paired[:, 0])
    odd_moved = jnp.where(pick_moved, paired[:, 0], paired[:, 1])
    table_pairs = legendre.reshape(own_rows, total // 2, 2, half_lats)
    pick_table = odd_order[:, None, None]
    even_table = jnp.where(pick_table, table_pairs[:, :, 1], table_pairs[:, :, 0])
    odd_table = jnp.where(pick_table, table_pairs[:, :, 0], table_pairs[:, :, 1])
    even_sum = jnp.einsum(
        "rqk,qrcs->rkcs", even_table, even_moved, preferred_element_type=jnp.float32
    )
    odd_sum = jnp.einsum("rqk,qrcs->rkcs", odd_table, odd_moved, preferred_element_type=jnp.float32)
    coeffs = jnp.concatenate([even_sum + odd_sum, even_sum - odd_sum], axis=1).astype(jnp.bfloat16)
    ordered = jnp.take(coeffs, lat_order, axis=1)
    arrived = lax.all_to_all(
        lax.all_to_all(ordered, "wave", split_axis=1, concat_axis=0, tiled=True),
        "lev",
        split_axis=1,
        concat_axis=0,
        tiled=True,
    )
    wave_list = (
        wave_order.reshape(wave_count, level_count, own_rows).transpose(1, 0, 2).reshape(total)
    )
    row_ids = flat_index * own_lats + jnp.arange(own_lats, dtype=jnp.int32)
    latitudes = jnp.take(lat_order, row_ids)
    by_latitude = jnp.moveaxis(arrived, 1, 0)
    factor = jnp.where(wave_list == 0, 1.0, 2.0).astype(jnp.float32)

    def grid_row(pieces):
        picked, latitude = pieces
        points = jnp.take(cycle_points, latitude % half_lats)
        cos_part, sin_part = trig_tables(wave_list, points, factor, LONW)
        trig_table = jnp.concatenate([cos_part, sin_part], axis=0)
        stacked = jnp.concatenate([picked[:, 0, :], picked[:, 1, :]], axis=0)
        result = jnp.einsum("ks,kj->sj", stacked, trig_table, preferred_element_type=jnp.float32)
        return result.astype(jnp.bfloat16)

    return lax.map(grid_row, (by_latitude, latitudes))


def solution(mesh):
    return jax.shard_map(
        shards,
        mesh=mesh,
        in_specs=(
            P(("wave", "lev"), None, None, None),
            P(("wave", "lev"), None, None),
            P(("wave", "lev"), None, None),
            P(),
            P(),
            P(),
        ),
        out_specs=P(("wave", "lev"), None, None),
        check_vma=False,
    )
```

profile of v0, /device:TPU:0, one launch (start us, length us, event | category | flops | bytes accessed | tf_op | source)
XLA Modules:
  0.0 1158.3 jit_solution(9919021062824959584)
XLA Ops:
  0.0 0.0 copy-start
  0.0 0.8 broadcast_compare_fusion.1
  0.8 0.8 broadcast_compare_fusion
  1.7 0.5 copy.57
  2.2 0.0 copy-done
  2.2 25.5 %multiply_convert_fusion = bf16[48,1536,2,64]{1,3,2,0:T(8,128)(2,1)} fusion(f32[48,1536,2]{1,2,0:T(2,128)S(1)} %copy.57, bf16[48,1536,2,137]{1,2,3,0:T(2,128)(2,1)} %param.6, bf16[48,64,137]{2,1,0:T(8,128)(2,1)S(1)} %copy-done), kind=kOutput, calls=%fused_computation.3 | convolution fusion | flops 2604662784 | bytes 60708864 | tf_op jit(solution)/shard_map/nrcl,nsl->nrcs/dot_general | solution.py:40
  27.7 77.5 %copy.58 = bf16[48,1536,2,64]{3,2,0,1:T(2,128)(2,1)} copy(bf16[48,1536,2,64]{1,3,2,0:T(8,128)(2,1)} %multiply_convert_fusion) | data formatting | bytes 37748736 | tf_op jit(solution)/shard_map/convert_element_type | solution.py:41
  105.2 34.2 %reshape.378 = bf16[16,2,294912]{2,1,0:T(2,128)(2,1)} reshape(bf16[1536,48,2,64]{3,2,1,0:T(2,128)(2,1)} %bitcast.94) | data formatting | bytes 37748736
  139.4 414.3 %all_to_all.66 = bf16[16,2,294912]{2,1,0:T(2,128)(2,1)} all-to-all(bf16[16,2,294912]{2,1,0:T(2,128)(2,1)} %reshape.378), channel_id=1, replica_groups=mesh['wave'=16,'lev'=2] {'wave'}, dimensions={0} | all-to-all | bytes 37748736 | tf_op jit(solution)/shard_map/all_to_all | solution.py:44
  553.7 33.8 %reshape.379 = bf16[1536,48,2,64]{3,2,1,0:T(2,128)(2,1)} reshape(bf16[16,2,294912]{2,1,0:T(2,128)(2,1)} %all_to_all.66) | data formatting | bytes 37748736
  587.5 80.9 %copy.59 = bf16[48,16,96,2,64]{2,4,3,0,1:T(8,128)(2,1)} copy(bf16[48,16,96,2,64]{4,3,0,2,1:T(2,128)(2,1)} %bitcast.95) | data formatting | bytes 37748736 | tf_op jit(solution)/shard_map/all_to_all | solution.py:44
  668.5 33.8 %copy.60 = bf16[768,96,2,64]{0,3,2,1:T(8,128)(2,1)} copy(bf16[768,96,2,64]{1,3,2,0:T(8,128)(2,1)} %bitcast.97) | data formatting | bytes 37748736 | tf_op jit(solution)/shard_map/all_to_all | solution.py:44
  702.3 0.0 copy-start.6
  702.3 0.0 copy-start.5
  702.3 0.0 copy-start.4
  702.3 10.8 all-to-all-start.1
  713.1 0.0 copy-done.6
  713.1 0.6 dynamic-slice.4
  714.4 0.0 copy-done.5
  714.4 0.6 dynamic-slice.5
  715.6 0.0 copy-done.4
  715.6 0.1 reshape.308
  715.7 10.6 copy.54
  726.3 0.1 fusion.40
  726.4 4.8 select_bitcast_fusion
  731.2 5.2 copy.73
  736.4 5.2 copy.72
  741.6 0.1 reshape.309
  741.8 3.4 fusion.37
  745.2 5.2 fusion.29
  750.4 168.6 %all-to-all-done.1 = bf16[768,96,2,64]{0,3,2,1:T(8,128)(2,1)} async-done(((bf16[768,96,2,64]{0,3,2,1:T(8,128)(2,1)}), bf16[768,96,2,64]{0,3,2,1:T(8,128)(2,1)}, u32[]{:S(2)}, u32[]{:S(2)}) %all-to-all-start.1) | async-done | bytes 18874400 | tf_op jit(solution)/shard_map/all_to_all | solution.py:43
  918.9 68.7 %reshape.307 = bf16[2,16,48,48,2,64]{2,1,5,4,3,0:T(8,128)(2,1)} reshape(bf16[2,768,48,2,64]{1,4,3,2,0:T(8,128)(2,1)} %bitcast.10) | data formatting | bytes 37748736 | tf_op jit(solution)/shard_map/reshape | solution.py:50
  987.7 59.8 %copy.61 = bf16[16,2,48,48,2,64]{5,3,4,2,1,0:T(8,128)(2,1)} copy(bf16[16,2,48,48,2,64]{2,0,5,4,3,1:T(8,128)(2,1)} %bitcast.93) | data formatting | bytes 37748736 | tf_op jit(solution)/shard_map/transpose | solution.py:51
  1047.4 25.8 %broadcast_select_fusion = (bf16[768,48,2,64]{3,1,2,0:T(8,128)(2,1)}, bf16[768,48,2,64]{3,1,2,0:T(8,128)(2,1)}) fusion(pred[48]{0:T(512)(128)(4,1)S(1)} %fusion.40, bf16[768,2,48,2,64]{4,2,3,1,0:T(8,128)(2,1)} %bitcast.96), kind=kLoop, calls=%fused_computation.10 | loop fusion | flops 9437184 | bytes 37748784 | tf_op jit(solution)/shard_map/jit(_where)/select_n | solution.py:57
  1073.3 19.1 %fusion.2 = f32[48,16,2,64]{3,1,2,0:T(8,128)S(1)} fusion(bf16[48,768,16,1]{1,2,3,0:T(8,128)(2,1)S(1)} %copy.73, bf16[768,48,2,64]{3,1,2,0:T(8,128)(2,1)} %get-tuple-element.48), kind=kOutput, calls=%fused_computation.6 | convolution fusion | flops 150994944 | bytes 11010048 | tf_op jit(solution)/shard_map/rqk,qrcs->rkcs/dot_general | solution.py:65
  1092.4 0.0 copy-start.2
  1092.4 0.0 copy-start.3
  1092.4 14.0 %add_convert_fusion = (bf16[48,16,2,64]{3,1,2,0:T(8,128)(2,1)S(1)}, bf16[48,16,2,64]{3,1,2,0:T(8,128)(2,1)S(1)}) fusion(f32[48,16,2,64]{3,1,2,0:T(8,128)S(1)} %fusion.2, bf16[48,768,16,1]{1,2,3,0:T(8,128)(2,1)S(1)} %copy.72, bf16[768,48,2,64]{3,1,2,0:T(8,128)(2,1)} %get-tuple-element.49), kind=kOutput, calls=%fused_computation.32 | convolution fusion | flops 151388160 | bytes 11403264 | tf_op jit(solution)/shard_map/rqk,qrcs->rkcs/dot_general | solution.py:62
  1106.4 0.2 pad_maximum_fusion
  1106.6 0.5 copy.67
  1107.1 0.7 gather_fusion
  1107.9 0.1 fusion.44
  1108.0 1.3 reshape.380
  1109.3 6.2 all-to-all-start.2
  1115.5 0.0 copy-done.2
  1115.5 0.0 copy-done.3
  1115.5 9.7 multiply_subtract_fusion
  1125.2 2.5 all-to-all-done.2
  1127.7 0.5 reshape.381
  1128.2 1.0 copy.68
  1129.2 2.0 all_to_all.58
  1131.2 3.5 all-to-all-start.3
  1134.6 0.0 copy-start.1
  1134.6 15.1 %fusion.12 = (bf16[1536,2048]{0,1:T(8,128)(2,1)}, bf16[1536,2048]{0,1:T(8,128)(2,1)}) fusion(f32[1536,32,64]{0,2,1:T(8,128)} %get-tuple-element.55, f32[1536]{0:T(1024)S(1)} %get-tuple-element.63, f32[1536,32,64]{0,2,1:T(8,128)} %get-tuple-element.54, f32[1536]{0:T(1024)S(1)} %get-tuple-element.62), kind=kLoop, calls=%fused_computation.17 | loop fusion | flops 12582912 | bytes 37761024 | tf_op jit(solution)/shard_map/while/body/eval_jaxpr/convert_element_type | solution.py:22
  1149.7 0.0 all-to-all-done.3
  1149.7 0.4 copy.69
  1150.2 0.2 squeeze.38
  1150.4 7.6 fusion.17
  1158.0 0.0 copy-done.1
  (9 shorter events, 0.1 us)
Async XLA Ops:
  0.0 2.2 copy-start
  702.3 10.8 copy-start.6
  702.3 12.1 %copy-start.5 = (s32[16]{0:T(128)S(1)}, s32[16]{0:T(128)}, u32[]{:S(2)}) copy-start(s32[16]{0:T(128)} %param.11) | copy-start | bytes 196
  702.3 13.3 %copy-start.4 = (s32[1536]{0:T(1024)S(1)}, s32[1536]{0:T(1024)}, u32[]{:S(2)}) copy-start(s32[1536]{0:T(1024)} %param.9) | copy-start | bytes 18436
  702.3 216.7 %all-to-all-start.1 = ((bf16[768,96,2,64]{0,3,2,1:T(8,128)(2,1)}), bf16[768,96,2,64]{0,3,2,1:T(8,128)(2,1)}, u32[]{:S(2)}, u32[]{:S(2)}) async-start(bf16[768,96,2,64]{0,3,2,1:T(8,128)(2,1)} %copy.60), calls=%async_computation.1 | async-start | bytes 37748736 | tf_op jit(solution)/shard_map/all_to_all | solution.py:43
  1092.4 23.1 %copy-start.2 = (f32[1536,32]{0,1:T(8,128)S(1)}, f32[1536,32]{0,1:T(8,128)}, u32[]{:S(2)}) copy-start(f32[1536,32]{0,1:T(8,128)} %get-tuple-element.60) | copy-start | bytes 589828
  1092.4 23.2 %copy-start.3 = (f32[1536,32]{0,1:T(8,128)S(1)}, f32[1536,32]{0,1:T(8,128)}, u32[]{:S(2)}) copy-start(f32[1536,32]{0,1:T(8,128)} %get-tuple-element.61) | copy-start | bytes 589828
  1109.3 18.4 %all-to-all-start.2 = ((bf16[16,2,6144]{2,1,0:T(2,128)(2,1)}), bf16[16,2,6144]{2,1,0:T(2,128)(2,1)S(1)}, u32[]{:S(2)}, u32[]{:S(2)}) async-start(bf16[16,2,6144]{2,1,0:T(2,128)(2,1)} %reshape.380), calls=%async_computation.2 | async-start | bytes 786432 | tf_op jit(solution)/shard_map/all_to_all | solution.py:69
  1131.2 18.6 %all-to-all-start.3 = ((bf16[768,2,2,64]{0,3,2,1:T(8,128)(2,1)}), bf16[768,2,2,64]{0,3,2,1:T(8,128)(2,1)S(1)}, u32[]{:S(2)}, u32[]{:S(2)}) async-start(bf16[768,2,2,64]{0,3,2,1:T(8,128)(2,1)} %all_to_all.58), calls=%async_computation.3 | async-start | bytes 786432 | tf_op jit(solution)/shard_map/all_to_all | solution.py:68
  1134.6 23.4 %copy-start.1 = (bf16[48,64,137]{2,1,0:T(8,128)(2,1)S(1)}, bf16[48,64,137]{2,1,0:T(8,128)(2,1)}, u32[]{:S(2)}) copy-start(bf16[48,64,137]{2,1,0:T(8,128)(2,1)} %param.7) | copy-start | bytes 2525188
where the time goes:
time: 1180 us; the launch traced here: 1160 us
  local copies, waits for them, and re-layouts  418 us (35%)
  blocking collectives  414 us (35%)
  waiting for transfers between devices  171 us (14%)
  other arithmetic  66.2 us (6%)
  matrix products  66.2 us (6%)
  starting transfers between devices  20.4 us (2%)
    all_to_all x1, blocking collectives, shards(): lax.all_to_all(slab, 'wave', split_axis=1, concat_axis=0, tiled=True)  414 us
    all_to_all x1, waiting for transfers between devices, shards(): lax.all_to_all(lax.all_to_all(slab, 'wave', split_axis=1, concat_axis=0,...  169 us
    all_to_all x2, local copies, waits for them, and re-layouts, shards(): lax.all_to_all(slab, 'wave', split_axis=1, concat_axis=0, tiled=True)  115 us
    unnamed x19, local copies, waits for them, and re-layouts  80.4 us
    convert_element_type x1, local copies, waits for them, and re-layouts, shards(): slab = (produced * weights[:, :, :, None]).astype(jnp.bfloat16)  77.5 us
    reshape x1, local copies, waits for them, and re-layouts, shards(): moved.reshape(level_count, wave_count, own_totals, own_rows, 2, slab_levels)  68.7 us
    transpose x1, local copies, waits for them, and re-layouts, shards(): jnp.transpose(moved, (1, 0, 2, 3, 4, 5))  59.8 us
    select_n x1, other arithmetic, shards(): odd_moved = jnp.where(pick_moved, paired[:, 0], paired[:, 1])  25.8 us
  transfers between devices with their start and end apart: 3, of which 2 were waited for; matrix products, arithmetic and copies ran while one was open for 5% of the time, Pallas kernels for 0%

commit v1 on v0

--- a/solution.py
+++ b/solution.py
@@ -1,6 +1,10 @@
+import functools
+
 import jax
 import jax.numpy as jnp
 from jax import lax
+from jax.experimental import pallas as pl
+from jax.experimental.pallas import tpu as pltpu
 from jax.sharding import PartitionSpec as P
 
 LONW = 2048
@@ -23,7 +27,7 @@
     return (cos_part, sin_part)
 
 
-def shards(control, covariance, legendre, wave_order, lat_order, cycle_points):
+def exchange_slab(control, covariance, legendre, wave_order, lat_order, cycle_points):
     wave_count = lax.axis_size("wave")
     level_count = lax.axis_size("lev")
     own_totals = control.shape[0]
@@ -92,6 +96,137 @@
     return lax.map(grid_row, (by_latitude, latitudes))
 
 
+GROUP = 8
+BLOCK = 128
+
+
+def partial_kernel(lat_ref, slab_ref, table_ref, mask_ref, out_ref, turned, signed):
+    totals, pairs, block = slab_ref.shape
+    half = table_ref.shape[1]
+    lats = out_ref.shape[0]
+    depth = totals * GROUP
+
+    def turn(n, carry):
+        flipped = slab_ref[n].astype(jnp.float32).T
+        start = pl.multiple_of(n * GROUP, GROUP)
+        turned[:, pl.ds(start, GROUP), :] = flipped.reshape(block // GROUP, GROUP, pairs)
+        return carry
+
+    lax.fori_loop(0, totals, turn, 0, unroll=2)
+    same = lax.broadcasted_iota(jnp.int32, (GROUP, depth), 1) % GROUP == lax.broadcasted_iota(
+        jnp.int32, (GROUP, depth), 0
+    )
+
+    def group_sum(g):
+        table = table_ref[g].astype(jnp.float32)
+        masks = mask_ref[g]
+        signed[pl.ds(0, half), :] = table * masks[0:1, :]
+        signed[pl.ds(half, half), :] = table * masks[1:2, :]
+        rows = []
+        for t in range(lats):
+            row = signed[pl.ds(lat_ref[t], 1), :]
+            rows.append(jnp.where(same, row, 0.0))
+        left = jnp.concatenate(rows, axis=0).astype(jnp.bfloat16)
+        right = turned[g].astype(jnp.bfloat16)
+        total = jnp.dot(left, right, preferred_element_type=jnp.float32)
+        return total.reshape(lats, GROUP, pairs)
+
+    def pair_of_groups(h, carry):
+        both = jnp.concatenate([group_sum(2 * h), group_sum(2 * h + 1)], axis=1)
+        start = pl.multiple_of(h * 2 * GROUP, 2 * GROUP)
+        out_ref[:, pl.ds(start, 2 * GROUP), :] = both.astype(jnp.bfloat16)
+        return carry
+
+    lax.fori_loop(0, block // (2 * GROUP), pair_of_groups, 0)
+
+
+def partial_sums(lat_order, slab, table, masks):
+    totals, pairs, rows = slab.shape
+    lats = lat_order.shape[0]
+    half = table.shape[1]
+    depth = totals * GROUP
+    groups = BLOCK // GROUP
+    return pl.pallas_call(
+        partial_kernel,
+        grid_spec=pltpu.PrefetchScalarGridSpec(
+            num_scalar_prefetch=1,
+            grid=(rows // BLOCK,),
+            in_specs=[
+                pl.BlockSpec((totals, pairs, BLOCK), lambda b, lat: (0, 0, b)),
+                pl.BlockSpec((groups, half, depth), lambda b, lat: (b, 0, 0)),
+                pl.BlockSpec((groups, 2, depth), lambda b, lat: (b, 0, 0)),
+            ],
+            out_specs=pl.BlockSpec((lats, BLOCK, pairs), lambda b, lat: (0, b, 0)),
+            scratch_shapes=[
+                pltpu.VMEM((groups, depth, pairs), jnp.float32),
+                pltpu.VMEM((2 * half, depth), jnp.float32),
+            ],
+        ),
+        out_shape=jax.ShapeDtypeStruct((lats, rows, pairs), jnp.bfloat16),
+        compiler_params=pltpu.CompilerParams(vmem_limit_bytes=40 * 1024 * 1024),
+        cost_estimate=pl.CostEstimate(
+            flops=2 * rows * GROUP * totals * lats * pairs,
+            bytes_accessed=2 * rows * pairs * (totals + lats),
+            transcendentals=0,
+        ),
+    )(lat_order, slab, table, masks)
+
+
+def reduce_partials(control, covariance, legendre, wave_order, lat_order, cycle_points):
+    device_count = lax.axis_size("wave") * lax.axis_size("lev")
+    own_totals = control.shape[0]
+    total = control.shape[1]
+    own_rows = legendre.shape[0]
+    half_lats = legendre.shape[2]
+    flat_index = lax.axis_index(("wave", "lev"))
+    total_ids = flat_index * own_totals + jnp.arange(own_totals, dtype=jnp.int32)
+
+    table = legendre.reshape(own_rows // GROUP, GROUP, device_count, own_totals, half_lats)
+    table = jnp.transpose(table, (2, 0, 4, 3, 1)).reshape(
+        device_count, own_rows // GROUP, half_lats, own_totals * GROUP
+    )
+    table = lax.all_to_all(table, ("wave", "lev"), split_axis=0, concat_axis=0, tiled=True)
+    table = table.reshape(total // GROUP, half_lats, own_totals * GROUP)
+
+    orders = wave_order.reshape(total // GROUP, 1, GROUP)
+    usable = total_ids[None, :, None] >= orders
+    sign = jnp.where((total_ids[None, :, None] + orders) % 2 == 1, -1.0, 1.0)
+    masks = jnp.stack([jnp.where(usable, 1.0, 0.0), jnp.where(usable, sign, 0.0)], axis=1)
+    masks = masks.reshape(total // GROUP, 2, own_totals * GROUP).astype(jnp.float32)
+
+    produced = jnp.einsum("nrcl,nsl->ncsr", control, covariance, preferred_element_type=jnp.float32)
+    slab = produced.astype(jnp.bfloat16)
+    slab_levels = slab.shape[2]
+    slab = slab.reshape(own_totals, 2 * slab_levels, total)
+    partial = partial_sums(lat_order, slab, table, masks)
+    coeffs = lax.psum_scatter(partial, ("wave", "lev"), scatter_dimension=0, tiled=True)[0]
+    latitude = jnp.take(lat_order, flat_index)
+    return fourier(coeffs, latitude, wave_order, cycle_points, half_lats, slab_levels)
+
+
+def fourier(coeffs, latitude, wave_order, cycle_points, half_lats, slab_levels):
+    factor = jnp.where(wave_order == 0, 1.0, 2.0).astype(jnp.float32)
+    points = jnp.take(cycle_points, latitude % half_lats)
+    cos_part, sin_part = trig_tables(wave_order, points, factor, LONW)
+    real = coeffs[:, :slab_levels]
+    imag = jnp.where((wave_order > 0)[:, None], coeffs[:, slab_levels:], 0)
+    stacked = jnp.concatenate([real, imag], axis=0)
+    trig_table = jnp.concatenate([cos_part, sin_part], axis=0)
+    result = jnp.einsum("ks,kj->sj", stacked, trig_table, preferred_element_type=jnp.float32)
+    return result.astype(jnp.bfloat16)[None]
+
+
+def shards(*arrays):
+    control, legendre, lat_order = arrays[0], arrays[2], arrays[4]
+    own_totals, total = control.shape[:2]
+    devices = lax.axis_size("wave") * lax.axis_size("lev")
+    smaller = 2 * legendre.shape[2] < own_totals
+    fits = total % BLOCK == 0 and legendre.shape[0] % GROUP == 0 and lat_order.shape[0] == devices
+    if smaller and fits:
+        return reduce_partials(*arrays)
+    return exchange_slab(*arrays)
+
+
 def solution(mesh):
     return jax.shard_map(
         shards,

time: 1180 us -> 332 us (0.28); the launches traced: 1160 us -> 331 us
  blocking collectives: 414 us -> 0 us
  local copies, waits for them, and re-layouts: 418 us -> 33.1 us
  Pallas kernels: 0 us -> 60.7 us
  other arithmetic: 66.2 us -> 23.2 us
  matrix products: 66.2 us -> 30.9 us
  between operations: 1.84 us -> 15 us
  starting transfers between devices: 20.4 us -> 7.45 us
    all_to_all x1 -> x0, blocking collectives: 414 us -> none  [shards(): lax.all_to_all(slab, 'wave', split_axis=1, concat_axis=0, tiled=True)]
    all_to_all x3 -> x1, waiting for transfers between devices: 171 us -> 28.6 us  [reduce_partials(): lax.all_to_all(table, ('wave', 'lev'), split_axis=0, concat_axis=0, tiled...]
    reduce_scatter x0 -> x1, waiting for transfers between devices: none -> 132 us  [reduce_partials(): lax.psum_scatter(partial, ('wave', 'lev'), scatter_dimension=0, tiled=True)]
    all_to_all x5 -> x0, local copies, waits for them, and re-layouts: 118 us -> none  [the longest x2 115 us: shards(): lax.all_to_all(slab, 'wave', split_axis=1, concat_axis=0, tiled=True)]
    unnamed x19 -> x10, local copies, waits for them, and re-layouts: 80.4 us -> 0.02 us
    convert_element_type x2 -> x0, local copies, waits for them, and re-layouts: 78 us -> none  [the longest x1 77.5 us: shards(): slab = (produced * weights[:, :, :, None]).astype(jnp.bfloat16)]
    pallas_call x0 -> x1, Pallas kernels: none -> 60.7 us  [partial_sums(): pl.pallas_call(partial_kernel, grid_spec=pltpu.PrefetchScalarGridSpec(num...]
    transpose x2 -> x0, local copies, waits for them, and re-layouts: 59.8 us -> none  [the longest x1 59.8 us: shards(): jnp.transpose(moved, (1, 0, 2, 3, 4, 5))]
  transfers between devices with their start and end apart: 3 -> 2, of which waited for: 2 -> 2; matrix products, arithmetic and copies ran while one was open for 5% -> 14% of each run, Pallas kernels for 0% -> 0%
where the time goes in v1:
time: 332 us; the launch traced here: 331 us
  waiting for transfers between devices  160 us (48%)
  Pallas kernels  60.7 us (18%)
  local copies, waits for them, and re-layouts  33.1 us (10%)
  matrix products  30.9 us (9%)
  other arithmetic  23.2 us (7%)
  between operations  15 us (5%)
  starting transfers between devices  7.45 us (2%)
    reduce_scatter x1, waiting for transfers between devices, reduce_partials(): lax.psum_scatter(partial, ('wave', 'lev'), scatter_dimension=0, tiled=True)  132 us
    pallas_call x1, Pallas kernels, partial_sums(): pl.pallas_call(partial_kernel, grid_spec=pltpu.PrefetchScalarGridSpec(num...  60.7 us
    all_to_all x1, waiting for transfers between devices, reduce_partials(): lax.all_to_all(table, ('wave', 'lev'), split_axis=0, concat_axis=0, tiled...  28.6 us
    dot_general x1, matrix products, reduce_partials(): jnp.einsum('nrcl,nsl->ncsr', control, covariance, preferred_element_type=...  23.2 us
    reshape x2, local copies, waits for them, and re-layouts, reduce_partials(): legendre.reshape(own_rows // GROUP, GROUP, device_count, own_totals, half...  21.4 us
    reshape x1, local copies, waits for them, and re-layouts, reduce_partials(): jnp.transpose(table, (2, 0, 4, 3, 1))  9.78 us
    convert_element_type x1, other arithmetic, trig_tables(): sin_part = (-factor[:, None] * sine).astype(jnp.bfloat16)  7.97 us
    dot_general x1, matrix products, fourier(): jnp.einsum('ks,kj->sj', stacked, trig_table, preferred_element_type=jnp.f...  7.63 us
  transfers between devices with their start and end apart: 2, of which 2 were waited for; matrix products, arithmetic and copies ran while one was open for 14% of the time, Pallas kernels for 0%

profile of v1, /device:TPU:0, one launch (start us, length us, event | category | flops | bytes accessed | tf_op | source)
XLA Modules:
  0.0 330.8 jit_solution(12507934567172187903)
XLA Ops:
  6.5 0.0 copy-start
  6.5 9.5 %reshape.292 = bf16[6,8,32,48,16]{3,2,4,1,0:T(8,128)(2,1)} reshape(bf16[48,1536,16]{1,2,0:T(8,128)(2,1)} %param.8) | data formatting | bytes 4718592 | tf_op jit(solution)/shard_map/reshape | solution.py:184
  16.1 0.0 copy-start.3
  16.1 11.9 %copy.16 = bf16[6,8,32,48,16]{2,1,3,4,0:T(8,128)(2,1)} copy(bf16[6,8,32,48,16]{3,2,4,1,0:T(8,128)(2,1)} %reshape.292) | data formatting | bytes 4718592 | tf_op jit(solution)/shard_map/reshape | solution.py:184
  27.9 9.8 %copy.17 = bf16[32,6,16,384]{3,2,1,0:T(8,128)(2,1)} copy(bf16[32,6,16,384]{0,3,2,1:T(8,128)(2,1)} %bitcast.32) | data formatting | bytes 4718592 | tf_op jit(solution)/shard_map/reshape | solution.py:185
  37.7 7.4 %all-to-all-start = ((bf16[32,6,16,384]{3,2,1,0:T(8,128)(2,1)}), bf16[32,6,16,384]{3,2,1,0:T(8,128)(2,1)}, u32[]{:S(2)}, u32[]{:S(2)}) async-start(bf16[32,6,16,384]{3,2,1,0:T(8,128)(2,1)} %copy.17), calls=%async_computation | async-start | bytes 4718592 | tf_op jit(solution)/shard_map/all_to_all | solution.py:188
  45.1 0.0 reduce-scatter.2.cloned.1.call-start
  45.2 0.1 ge.42
  45.3 0.1 ge.43
  45.4 0.0 copy-done.3
  45.4 0.1 ge.45
  45.5 0.1 copy.18
  45.6 0.2 copy.19
  45.8 1.3 compare_select_fusion.4
  47.1 0.5 pad_maximum_fusion.mask_ref
  47.6 0.0 copy-done
  47.6 0.0 copy-start.2
  47.7 23.2 %fusion.2 = bf16[48,64,1536,2]{2,1,3,0:T(8,128)(2,1)} fusion(bf16[48,1536,2,137]{1,2,3,0:T(2,128)(2,1)} %param.6, bf16[48,64,137]{2,1,0:T(8,128)(2,1)S(1)} %copy-done), kind=kOutput, calls=%fused_computation.2 | convolution fusion | flops 2595225600 | bytes 60119040 | tf_op jit(solution)/shard_map/nrcl,nsl->ncsr/dot_general | solution.py:197
  70.9 28.6 %all-to-all-done = bf16[32,6,16,384]{3,2,1,0:T(8,128)(2,1)} async-done(((bf16[32,6,16,384]{3,2,1,0:T(8,128)(2,1)}), bf16[32,6,16,384]{3,2,1,0:T(8,128)(2,1)}, u32[]{:S(2)}, u32[]{:S(2)}) %all-to-all-start) | async-done | bytes 2359328 | tf_op jit(solution)/shard_map/all_to_all | solution.py:188
  99.5 0.0 copy-done.2
  99.5 60.7 %shard_map.64 = bf16[32,1536,128]{2,1,0:T(8,128)(2,1)} custom-call(s32[32]{0:T(128)S(1)} %copy-done.2, bf16[48,128,1536]{2,1,0:T(8,128)(2,1)} %bitcast.31, bf16[192,16,384]{2,1,0:T(8,128)(2,1)} %bitcast.6.table_ref, f32[192,2,384]{2,1,0:T(2,128)S(1)} %pad_maximum_fusion.mask_ref), custom_call_target="tpu_custom_call" | custom-call | flops 4831838208 | bytes 31457280 | tf_op jit(solution)/shard_map/pallas_call | solution.py:149
  160.2 0.0 copy-start.4
  160.2 0.0 reduce-scatter.2.cloned.1.call-update
  160.3 0.7 dynamic-slice.4
  161.6 0.0 copy-done.4
  161.6 0.7 dynamic-slice.5
  163.1 2.7 fusion.35
  165.8 5.2 %fusion.26 = (f32[1536,64]{0,1:T(8,128)S(1)}, f32[1536,64]{0,1:T(8,128)S(1)}) fusion(f32[]{:T(128)S(6)} %div.3, s32[]{:T(128)S(6)} %select_n.119, s32[1536]{0:T(1024)S(1)} %copy-done.3, pred[]{:T(512)S(6)} %lt.53), kind=kLoop, calls=%fused_computation.34 | loop fusion | flops 983040 | bytes 792585 | tf_op jit(solution)/shard_map/cos | solution.py:21
  170.9 4.0 %multiply_subtract_fusion = (f32[1536,32,64]{0,2,1:T(8,128)S(1)}, f32[1536,32,64]{0,2,1:T(8,128)S(1)}) fusion(f32[1536,64]{0,1:T(8,128)S(1)} %get-tuple-element.38, f32[1536,32]{0,1:T(8,128)S(1)} %get-tuple-element.34, f32[1536,64]{0,1:T(8,128)S(1)} %get-tuple-element.37, f32[1536,32]{0,1:T(8,128)S(1)} %get-tuple-element.33), kind=kLoop, calls=%fused_computation.12 | loop fusion | flops 18874368 | bytes 26345472 | tf_op jit(solution)/shard_map/sub | solution.py:23
  175.0 0.0 copy-start.1
  175.0 8.0 %fusion.9 = (bf16[1536,2048]{0,1:T(8,128)(2,1)}, bf16[1536,2048]{0,1:T(8,128)(2,1)}) fusion(f32[1536,32,64]{0,2,1:T(8,128)S(1)} %get-tuple-element.28, f32[1536]{0:T(1024)S(1)} %get-tuple-element.36, f32[1536,32,64]{0,2,1:T(8,128)S(1)} %get-tuple-element.27, f32[1536]{0:T(1024)S(1)} %get-tuple-element.35), kind=kLoop, calls=%fused_computation.8 | loop fusion | flops 12582912 | bytes 37761024 | tf_op jit(solution)/shard_map/convert_element_type | solution.py:26
  183.0 131.9 %reduce-scatter.2.cloned.1.call-done = bf16[1,1536,128]{2,1,0:T(8,128)(2,1)} async-done(((bf16[32,1536,128]{2,1,0:T(8,128)(2,1)}), bf16[1,1536,128]{2,1,0:T(8,128)(2,1)}) %reduce-scatter.2.cloned.1.call-update) | async-done | bytes 393232 | tf_op jit(solution)/shard_map/reduce_scatter | solution.py:202
  314.8 1.5 fusion.40
  316.3 7.6 %fusion.14 = bf16[1,64,2048]{2,1,0:T(8,128)(2,1)} fusion(bf16[1536,2048]{0,1:T(8,128)(2,1)} %get-tuple-element.39, bf16[1536,2048]{0,1:T(8,128)(2,1)} %get-tuple-element.40, bf16[1536,64]{1,0:T(8,128)(2,1)S(1)} %get-tuple-element.30, bf16[1536,64]{1,0:T(8,128)(2,1)S(1)} %get-tuple-element.29), kind=kOutput, calls=%fused_computation.14 | convolution fusion | flops 831389696 | bytes 13238272 | tf_op jit(solution)/shard_map/ks,kj->sj/dot_general | solution.py:215
  323.9 0.0 copy-done.1
  (5 shorter events, 0.1 us)
Async XLA Ops:
  6.5 41.1 %copy-start = (bf16[48,64,137]{2,1,0:T(8,128)(2,1)S(1)}, bf16[48,64,137]{2,1,0:T(8,128)(2,1)}, u32[]{:S(2)}) copy-start(bf16[48,64,137]{2,1,0:T(8,128)(2,1)} %param.7) | copy-start | bytes 2525188
  16.1 29.3 %copy-start.3 = (s32[1536]{0:T(1024)S(1)}, s32[1536]{0:T(1024)}, u32[]{:S(2)}) copy-start(s32[1536]{0:T(1024)} %param.9) | copy-start | bytes 18436
  37.7 61.8 %all-to-all-start = ((bf16[32,6,16,384]{3,2,1,0:T(8,128)(2,1)}), bf16[32,6,16,384]{3,2,1,0:T(8,128)(2,1)}, u32[]{:S(2)}, u32[]{:S(2)}) async-start(bf16[32,6,16,384]{3,2,1,0:T(8,128)(2,1)} %copy.17), calls=%async_computation | async-start | bytes 4718592 | tf_op jit(solution)/shard_map/all_to_all | solution.py:188
  45.1 269.7 %reduce-scatter.2.cloned.1.call-start = ((), (), s32[]{:S(2)}) async-start(), calls=%async_computation.2 | async-start | bytes 12976128 | tf_op jit(solution)/shard_map/reduce_scatter | solution.py:202
  47.6 51.9 %copy-start.2 = (s32[32]{0:T(128)S(1)}, s32[32]{0:T(128)}, u32[]{:S(2)}) copy-start(s32[32]{0:T(128)} %lat_ref.1) | copy-start | bytes 388
  160.2 1.4 copy-start.4
  175.0 149.0 %copy-start.1 = (bf16[48,64,137]{2,1,0:T(8,128)(2,1)S(1)}, bf16[48,64,137]{2,1,0:T(8,128)(2,1)}, u32[]{:S(2)}) copy-start(bf16[48,64,137]{2,1,0:T(8,128)(2,1)} %param.7) | copy-start | bytes 2525188
Sparse Core Ops, SparseCore 0:
  160.4 154.3 reduce-scatter.1

commit v2 on v1

--- a/solution.py
+++ b/solution.py
@@ -1,7 +1,6 @@
-import functools
-
 import jax
 import jax.numpy as jnp
+import numpy as np
 from jax import lax
 from jax.experimental import pallas as pl
 from jax.experimental.pallas import tpu as pltpu
@@ -100,76 +99,191 @@
 BLOCK = 128
 
 
-def partial_kernel(lat_ref, slab_ref, table_ref, mask_ref, out_ref, turned, signed):
+def fused_kernel(
+    pick_ref, slab_ref, table_ref, mask_ref, out_ref,
+    turned, picked, part, from_core, from_first, from_second, from_z, send_sem, recv_sem,
+):
     totals, pairs, block = slab_ref.shape
-    half = table_ref.shape[1]
-    lats = out_ref.shape[0]
-    depth = totals * GROUP
-
-    def turn(n, carry):
-        flipped = slab_ref[n].astype(jnp.float32).T
-        start = pl.multiple_of(n * GROUP, GROUP)
-        turned[:, pl.ds(start, GROUP), :] = flipped.reshape(block // GROUP, GROUP, pairs)
-        return carry
-
-    lax.fori_loop(0, totals, turn, 0, unroll=2)
-    same = lax.broadcasted_iota(jnp.int32, (GROUP, depth), 1) % GROUP == lax.broadcasted_iota(
-        jnp.int32, (GROUP, depth), 0
-    )
-
-    def group_sum(g):
-        table = table_ref[g].astype(jnp.float32)
-        masks = mask_ref[g]
-        signed[pl.ds(0, half), :] = table * masks[0:1, :]
-        signed[pl.ds(half, half), :] = table * masks[1:2, :]
-        rows = []
-        for t in range(lats):
-            row = signed[pl.ds(lat_ref[t], 1), :]
-            rows.append(jnp.where(same, row, 0.0))
-        left = jnp.concatenate(rows, axis=0).astype(jnp.bfloat16)
-        right = turned[g].astype(jnp.bfloat16)
-        total = jnp.dot(left, right, preferred_element_type=jnp.float32)
-        return total.reshape(lats, GROUP, pairs)
-
-    def pair_of_groups(h, carry):
-        both = jnp.concatenate([group_sum(2 * h), group_sum(2 * h + 1)], axis=1)
-        start = pl.multiple_of(h * 2 * GROUP, 2 * GROUP)
-        out_ref[:, pl.ds(start, 2 * GROUP), :] = both.astype(jnp.bfloat16)
-        return carry
-
-    lax.fori_loop(0, block // (2 * GROUP), pair_of_groups, 0)
-
-
-def partial_sums(lat_order, slab, table, masks):
+    groups, half, depth = table_ref.shape
+    lats = pick_ref.shape[1]
+    blocks, z_count = part.shape[0], part.shape[4]
+    step = pl.program_id(0)
+    wave, y = lax.axis_index("wave"), lax.axis_index("lev")
+    core, x, z = wave % 2, (wave // 2) % 2, wave // 4
+
+    def z_other(k):
+        return lax.rem(z + k, z_count)
+
+    def hop(b, stage):
+        odd = b % 2
+        first = x + odd * (y - x)
+        second = y + odd * (x - y)
+        if stage == 0:
+            source, target = part.at[b, 1 - core], from_core.at[b]
+            device = (wave + 1 - 2 * core, y)
+        elif stage == 1:
+            source, target = part.at[b, core, 1 - first], from_first.at[b]
+            device = (wave + (1 - odd) * (2 - 4 * x), y + odd * (1 - 2 * y))
+        elif stage == 2:
+            source, target = part.at[b, core, first, 1 - second], from_second.at[b]
+            device = (wave + odd * (2 - 4 * x), y + (1 - odd) * (1 - 2 * y))
+        else:
+            k = stage - 2
+            source, target = part.at[b, core, first, second, z_other(k)], from_z.at[b, k - 1]
+            device = (z_other(k) * 4 + x * 2 + core, y)
+        return pltpu.make_async_remote_copy(
+            src_ref=source,
+            dst_ref=target,
+            send_sem=send_sem.at[b, stage],
+            recv_sem=recv_sem.at[b, stage],
+            device_id=device,
+            device_id_type=pl.DeviceIdType.MESH,
+        )
+
+    @pl.when(step == 0)
+    def _():
+        barrier = pltpu.get_barrier_semaphore()
+        partners = [(wave + 1 - 2 * core, y), (wave + 2 - 4 * x, y), (wave, 1 - y)]
+        partners += [(z_other(k) * 4 + x * 2 + core, y) for k in range(1, z_count)]
+        for partner in partners:
+            pl.semaphore_signal(
+                barrier, inc=1, device_id=partner, device_id_type=pl.DeviceIdType.MESH
+            )
+        pl.semaphore_wait(barrier, len(partners))
+
+    @pl.when(step < blocks)
+    def _():
+        def turn(n, carry):
+            flipped = slab_ref[n].astype(jnp.float32).T
+            start = pl.multiple_of(n * GROUP, GROUP)
+            turned[:, pl.ds(start, GROUP), :] = flipped.reshape(groups, GROUP, pairs)
+            return carry
+
+        lax.fori_loop(0, totals, turn, 0, unroll=4)
+        same = lax.broadcasted_iota(jnp.int32, (GROUP, depth), 1) % GROUP == lax.broadcasted_iota(
+            jnp.int32, (GROUP, depth), 0
+        )
+        pick = pick_ref[step % 2]
+
+        def group_sum(g, slot):
+            table = table_ref[g].astype(jnp.float32)
+            masks = mask_ref[g]
+            both = jnp.concatenate([table * masks[0:1, :], table * masks[1:2, :]], axis=0)
+            picked[slot] = jnp.dot(
+                pick, both.astype(jnp.bfloat16), preferred_element_type=jnp.float32
+            )
+            rows = []
+            for t in range(lats):
+                rows.append(jnp.where(same, picked[slot, t : t + 1, :], 0.0))
+            left = jnp.concatenate(rows, axis=0).astype(jnp.bfloat16)
+            right = turned[g].astype(jnp.bfloat16)
+            total = jnp.dot(left, right, preferred_element_type=jnp.float32)
+            return total.reshape(lats, GROUP, pairs)
+
+        def pair_of_groups(h, carry):
+            both = jnp.concatenate([group_sum(2 * h, 0), group_sum(2 * h + 1, 1)], axis=1)
+            both = both.astype(jnp.bfloat16).reshape(2, 2, 2, z_count, 2 * GROUP, pairs)
+            start = pl.multiple_of(h * 2 * GROUP, 2 * GROUP)
+            part[step, :, :, :, :, pl.ds(start, 2 * GROUP), :] = both
+            return carry
+
+        lax.fori_loop(0, groups // 2, pair_of_groups, 0)
+        hop(step, 0).start()
+
+    def add(to, arrived):
+        return (to.astype(jnp.float32) + arrived.astype(jnp.float32)).astype(jnp.bfloat16)
+
+    @pl.when((step >= 1) & (step < blocks + 1))
+    def _():
+        b = step - 1
+        hop(b, 0).wait()
+
+        def slab_add(i, carry):
+            part[b, core, i // 2, i % 2] = add(
+                part[b, core, i // 2, i % 2], from_core[b, i // 2, i % 2]
+            )
+            return carry
+
+        lax.fori_loop(0, 4, slab_add, 0)
+        hop(b, 1).start()
+
+    @pl.when((step >= 2) & (step < blocks + 2))
+    def _():
+        b = step - 2
+        first = x + (b % 2) * (y - x)
+        hop(b, 1).wait()
+
+        def slab_add(i, carry):
+            part[b, core, first, i] = add(part[b, core, first, i], from_first[b, i])
+            return carry
+
+        lax.fori_loop(0, 2, slab_add, 0)
+        hop(b, 2).start()
+
+    @pl.when((step >= 3) & (step < blocks + 3))
+    def _():
+        b = step - 3
+        first = x + (b % 2) * (y - x)
+        second = y + (b % 2) * (x - y)
+        hop(b, 2).wait()
+        part[b, core, first, second] = add(part[b, core, first, second], from_second[b])
+        for k in range(1, z_count):
+            hop(b, 2 + k).start()
+
+    @pl.when(step >= 4)
+    def _():
+        b = step - 4
+        first = x + (b % 2) * (y - x)
+        second = y + (b % 2) * (x - y)
+        total = part[b, core, first, second, z].astype(jnp.float32)
+        for k in range(1, z_count):
+            hop(b, 2 + k).wait()
+            total = total + from_z[b, k - 1].astype(jnp.float32)
+        start = pl.multiple_of(b * block, block)
+        out_ref[pl.ds(start, block), :] = total.astype(jnp.bfloat16)
+
+
+def reduced_sums(pick, slab, table, masks, z_count):
     totals, pairs, rows = slab.shape
-    lats = lat_order.shape[0]
+    lats = pick.shape[1]
     half = table.shape[1]
     depth = totals * GROUP
     groups = BLOCK // GROUP
+    blocks = rows // BLOCK
+    last = blocks - 1
+    tile = (BLOCK, pairs)
+    stages = 3 + z_count - 1
     return pl.pallas_call(
-        partial_kernel,
-        grid_spec=pltpu.PrefetchScalarGridSpec(
-            num_scalar_prefetch=1,
-            grid=(rows // BLOCK,),
-            in_specs=[
-                pl.BlockSpec((totals, pairs, BLOCK), lambda b, lat: (0, 0, b)),
-                pl.BlockSpec((groups, half, depth), lambda b, lat: (b, 0, 0)),
-                pl.BlockSpec((groups, 2, depth), lambda b, lat: (b, 0, 0)),
-            ],
-            out_specs=pl.BlockSpec((lats, BLOCK, pairs), lambda b, lat: (0, b, 0)),
-            scratch_shapes=[
-                pltpu.VMEM((groups, depth, pairs), jnp.float32),
-                pltpu.VMEM((2 * half, depth), jnp.float32),
-            ],
+        fused_kernel,
+        grid=(blocks + 4,),
+        in_specs=[
+            pl.BlockSpec((2, lats, 2 * half), lambda b: (0, 0, 0)),
+            pl.BlockSpec((totals, pairs, BLOCK), lambda b: (0, 0, jnp.minimum(b, last))),
+            pl.BlockSpec((groups, half, depth), lambda b: (jnp.minimum(b, last), 0, 0)),
+            pl.BlockSpec((groups, 2, depth), lambda b: (jnp.minimum(b, last), 0, 0)),
+        ],
+        out_specs=pl.BlockSpec((rows, pairs), lambda b: (0, 0)),
+        scratch_shapes=[
+            pltpu.VMEM((groups, depth, pairs), jnp.float32),
+            pltpu.VMEM((2, lats, depth), jnp.float32),
+            pltpu.VMEM((blocks, 2, 2, 2, z_count) + tile, jnp.bfloat16),
+            pltpu.VMEM((blocks, 2, 2, z_count) + tile, jnp.bfloat16),
+            pltpu.VMEM((blocks, 2, z_count) + tile, jnp.bfloat16),
+            pltpu.VMEM((blocks, z_count) + tile, jnp.bfloat16),
+            pltpu.VMEM((blocks, z_count - 1) + tile, jnp.bfloat16),
+            pltpu.SemaphoreType.DMA((blocks, stages)),
+            pltpu.SemaphoreType.DMA((blocks, stages)),
+        ],
+        out_shape=jax.ShapeDtypeStruct((rows, pairs), jnp.bfloat16),
+        compiler_params=pltpu.CompilerParams(
+            vmem_limit_bytes=44 * 1024 * 1024, collective_id=0, has_side_effects=True
         ),
-        out_shape=jax.ShapeDtypeStruct((lats, rows, pairs), jnp.bfloat16),
-        compiler_params=pltpu.CompilerParams(vmem_limit_bytes=40 * 1024 * 1024),
         cost_estimate=pl.CostEstimate(
             flops=2 * rows * GROUP * totals * lats * pairs,
-            bytes_accessed=2 * rows * pairs * (totals + lats),
+            bytes_accessed=2 * rows * pairs * totals,
             transcendentals=0,
         ),
-    )(lat_order, slab, table, masks)
+    )(pick, slab, table, masks)
 
 
 def reduce_partials(control, covariance, legendre, wave_order, lat_order, cycle_points):
@@ -198,8 +312,14 @@
     slab = produced.astype(jnp.bfloat16)
     slab_levels = slab.shape[2]
     slab = slab.reshape(own_totals, 2 * slab_levels, total)
-    partial = partial_sums(lat_order, slab, table, masks)
-    coeffs = lax.psum_scatter(partial, ("wave", "lev"), scatter_dimension=0, tiled=True)[0]
+    z_count = lax.axis_size("wave") // 4
+    owner = np.arange(device_count).reshape(z_count, 2, 2, 2)
+    owners = np.stack(
+        [owner.transpose(2, 1, 3, 0).reshape(-1), owner.transpose(2, 3, 1, 0).reshape(-1)]
+    )
+    wanted = lat_order[owners][:, :, None] == jnp.arange(2 * half_lats, dtype=jnp.int32)
+    pick = wanted.astype(jnp.bfloat16)
+    coeffs = reduced_sums(pick, slab, table, masks, z_count)
     latitude = jnp.take(lat_order, flat_index)
     return fourier(coeffs, latitude, wave_order, cycle_points, half_lats, slab_levels)
 
@@ -222,6 +342,7 @@
     devices = lax.axis_size("wave") * lax.axis_size("lev")
     smaller = 2 * legendre.shape[2] < own_totals
     fits = total % BLOCK == 0 and legendre.shape[0] % GROUP == 0 and lat_order.shape[0] == devices
+    fits = fits and lax.axis_size("lev") == 2 and lax.axis_size("wave") % 4 == 0
     if smaller and fits:
         return reduce_partials(*arrays)
     return exchange_slab(*arrays)

time: 332 us -> 209 us (0.63)
  waiting for transfers between devices: 160 us -> 0.01 us
  Pallas kernels: 60.7 us -> 109 us
  between operations: 15 us -> 1.57 us
  other arithmetic: 23.2 us -> 28.8 us
  matrix products: 30.9 us -> 27.5 us
    reduce_scatter x1 -> x0, waiting for transfers between devices: 132 us -> none  [reduce_partials(): lax.psum_scatter(partial, ('wave', 'lev'), scatter_dimension=0, tiled=True)]
    pallas_call x1, Pallas kernels: 60.7 us -> 109 us  [reduced_sums(): pl.pallas_call(fused_kernel, grid=(blocks + 4,), in_specs=[pl.BlockSpec((...]
    all_to_all x1, waiting for transfers between devices: 28.6 us -> 0.01 us  [reduce_partials(): lax.all_to_all(table, ('wave', 'lev'), split_axis=0, concat_axis=0, tiled...]
    convert_element_type x1, other arithmetic: 7.97 us -> 11.9 us  [trig_tables(): sin_part = (-factor[:, None] * sine).astype(jnp.bfloat16)]
  transfers between devices with their start and end apart: 2 -> 1, of which waited for: 2 -> 0; matrix products, arithmetic and copies ran while one was open for 14% -> 26% of each run, Pallas kernels for 0% -> 0%
where the time goes in v2:
time: 209 us; the launch traced here: 208 us
  Pallas kernels  109 us (52%)
  local copies, waits for them, and re-layouts  33.8 us (16%)
  other arithmetic  28.8 us (14%)
  matrix products  27.5 us (13%)
  starting transfers between devices  7.41 us (4%)
    pallas_call x1, Pallas kernels, reduced_sums(): pl.pallas_call(fused_kernel, grid=(blocks + 4,), in_specs=[pl.BlockSpec((...  109 us
    dot_general x1, matrix products, reduce_partials(): jnp.einsum('nrcl,nsl->ncsr', control, covariance, preferred_element_type=...  22.8 us
    reshape x2, local copies, waits for them, and re-layouts, reduce_partials(): legendre.reshape(own_rows // GROUP, GROUP, device_count, own_totals, half...  21.4 us
    convert_element_type x1, other arithmetic, trig_tables(): sin_part = (-factor[:, None] * sine).astype(jnp.bfloat16)  11.9 us
    reshape x1, local copies, waits for them, and re-layouts, reduce_partials(): jnp.transpose(table, (2, 0, 4, 3, 1))  9.73 us
    all_to_all x1, starting transfers between devices, reduce_partials(): lax.all_to_all(table, ('wave', 'lev'), split_axis=0, concat_axis=0, tiled...  7.41 us
    sub x1, other arithmetic, trig_tables(): cosine = (cos_c * cos_f - sin_c * sin_f).reshape(orders.shape[0], width)  6.81 us
    cos x1, other arithmetic, trig_tables(): cos_f = jnp.cos(fine_angle)[:, None, :]  5.18 us
  transfers between devices with their start and end apart: 1, of which 0 were waited for; matrix products, arithmetic and copies ran while one was open for 26% of the time, Pallas kernels for 0%

profile of v2, /device:TPU:0, one launch (start us, length us, event | category | flops | bytes accessed | tf_op | source)
XLA Modules:
  0.0 208.2 jit_solution(2763809291457171578)
XLA Ops:
  0.0 0.0 copy-start
  0.0 9.5 %reshape.293 = bf16[6,8,32,48,16]{3,2,4,1,0:T(8,128)(2,1)} reshape(bf16[48,1536,16]{1,2,0:T(8,128)(2,1)} %param.10) | data formatting | bytes 4718592 | tf_op jit(solution)/shard_map/reshape | solution.py:298
  9.5 0.0 copy-start.1
  9.5 0.0 copy-start.4
  9.5 0.0 copy-start.2
  9.5 0.0 copy-start.3
  9.5 11.9 %copy.18 = bf16[6,8,32,48,16]{2,1,3,4,0:T(8,128)(2,1)} copy(bf16[6,8,32,48,16]{3,2,4,1,0:T(8,128)(2,1)} %reshape.293) | data formatting | bytes 4718592 | tf_op jit(solution)/shard_map/reshape | solution.py:298
  21.4 9.7 %copy.19 = bf16[32,6,16,384]{3,2,1,0:T(8,128)(2,1)} copy(bf16[32,6,16,384]{0,3,2,1:T(8,128)(2,1)} %bitcast.31) | data formatting | bytes 4718592 | tf_op jit(solution)/shard_map/reshape | solution.py:299
  31.1 7.4 %all-to-all-start = ((bf16[32,6,16,384]{3,2,1,0:T(8,128)(2,1)}), bf16[32,6,16,384]{3,2,1,0:T(8,128)(2,1)}, u32[]{:S(2)}, u32[]{:S(2)}) async-start(bf16[32,6,16,384]{3,2,1,0:T(8,128)(2,1)} %copy.19), calls=%async_computation | async-start | bytes 4718592 | tf_op jit(solution)/shard_map/all_to_all | solution.py:302
  38.6 0.0 copy-done.1
  38.6 0.6 dynamic-slice.4
  39.8 0.0 copy-done.4
  39.8 0.6 dynamic-slice.5
  41.1 0.0 copy-done.2
  41.1 0.1 ge.45
  41.2 0.0 copy-done.3
  41.3 0.8 gather_fusion
  42.0 0.1 reshape.355
  42.1 0.1 fusion.38.pick_ref
  42.2 0.1 ge.42
  42.3 0.1 ge.43
  42.4 0.1 copy.20
  42.5 0.2 copy.21
  42.7 5.2 %fusion.26 = (f32[1536,64]{0,1:T(8,128)S(1)}, f32[1536,64]{0,1:T(8,128)S(1)}) fusion(f32[]{:T(128)S(6)} %div.3, s32[]{:T(128)S(6)} %select_n.123, s32[1536]{0:T(1024)S(1)} %copy-done.2, pred[]{:T(512)S(6)} %lt.53), kind=kLoop, calls=%fused_computation.34 | loop fusion | flops 983040 | bytes 792585 | tf_op jit(solution)/shard_map/cos | solution.py:20
  47.9 2.7 %fusion.35 = (f32[1536,32]{0,1:T(8,128)S(1)}, f32[1536,32]{0,1:T(8,128)S(1)}) fusion(f32[]{:T(128)S(6)} %div.3, s32[]{:T(128)S(6)} %select_n.123, s32[32]{0:T(128)S(1)} %iota_multiply_fusion, s32[1536]{0:T(1024)S(1)} %copy-done.2, pred[]{:T(512)S(6)} %lt.53), kind=kLoop, calls=%fused_computation.46 | loop fusion | flops 491520 | bytes 399497 | tf_op jit(solution)/shard_map/cos | solution.py:18
  50.6 1.3 compare_select_fusion.4
  51.9 0.5 pad_maximum_fusion.mask_ref
  52.4 6.8 %multiply_subtract_fusion = (f32[1536,32,64]{0,2,1:T(8,128)S(1)}, f32[1536,32,64]{0,2,1:T(8,128)}) fusion(f32[1536,64]{0,1:T(8,128)S(1)} %get-tuple-element.38, f32[1536,32]{0,1:T(8,128)S(1)} %get-tuple-element.34, f32[1536,64]{0,1:T(8,128)S(1)} %get-tuple-element.37, f32[1536,32]{0,1:T(8,128)S(1)} %get-tuple-element.33), kind=kLoop, calls=%fused_computation.13 | loop fusion | flops 18874368 | bytes 26345472 | tf_op jit(solution)/shard_map/sub | solution.py:22
  59.3 11.9 %fusion.9 = (bf16[1536,2048]{0,1:T(8,128)(2,1)}, bf16[1536,2048]{0,1:T(8,128)(2,1)}) fusion(f32[1536,32,64]{0,2,1:T(8,128)} %get-tuple-element.28, f32[1536]{0:T(1024)S(1)} %get-tuple-element.36, f32[1536,32,64]{0,2,1:T(8,128)S(1)} %get-tuple-element.27, f32[1536]{0:T(1024)S(1)} %get-tuple-element.35), kind=kLoop, calls=%fused_computation.9 | loop fusion | flops 12582912 | bytes 37761024 | tf_op jit(solution)/shard_map/convert_element_type | solution.py:25
  71.1 0.0 copy-done
  71.1 22.8 %fusion.2 = bf16[48,64,1536,2]{2,1,3,0:T(8,128)(2,1)} fusion(bf16[48,1536,2,137]{1,2,3,0:T(2,128)(2,1)} %param.8, bf16[48,64,137]{2,1,0:T(8,128)(2,1)S(1)} %copy-done), kind=kOutput, calls=%fused_computation.3 | convolution fusion | flops 2595225600 | bytes 60119040 | tf_op jit(solution)/shard_map/nrcl,nsl->ncsr/dot_general | solution.py:311
  94.0 0.0 all-to-all-done
  94.0 0.0 slice-start
  94.0 0.0 slice-start.2
  94.0 0.0 slice-start.1
  94.0 0.0 slice-start.3
  94.0 109.1 %shard_map.82 = bf16[1536,128]{1,0:T(8,128)(2,1)S(1)} custom-call(bf16[2,32,32]{2,1,0:T(8,128)(2,1)S(1)} %fusion.38.pick_ref, bf16[48,128,1536]{2,1,0:T(8,128)(2,1)} %bitcast.30, bf16[192,16,384]{2,1,0:T(8,128)(2,1)} %bitcast.6.table_ref, f32[192,2,384]{2,1,0:T(2,128)S(1)} %pad_maximum_fusion.mask_ref), custom_call_target="tpu_custom_call" | custom-call | flops 4831838208 | bytes 18874368 | tf_op jit(solution)/shard_map/pallas_call | solution.py:256
  203.1 0.4 fusion.41
  203.5 0.0 slice-done
  203.5 0.0 slice-done.2
  203.5 0.0 slice-done.1
  203.5 0.0 slice-done.3
  203.5 4.7 %fusion.14 = bf16[1,64,2048]{2,1,0:T(8,128)(2,1)} fusion(bf16[1536,2048]{0,1:T(8,128)(2,1)S(1)} %bitcast.33, bf16[1536,2048]{0,1:T(8,128)(2,1)S(1)} %bitcast.35, bf16[1536,64]{1,0:T(8,128)(2,1)S(1)} %get-tuple-element.30, bf16[1536,64]{1,0:T(8,128)(2,1)S(1)} %get-tuple-element.29), kind=kOutput, calls=%fused_computation.15 | convolution fusion | flops 831389696 | bytes 13238272 | tf_op jit(solution)/shard_map/ks,kj->sj/dot_general | solution.py:335
  (8 shorter events, 0.1 us)
Async XLA Ops:
  0.0 71.1 %copy-start = (bf16[48,64,137]{2,1,0:T(8,128)(2,1)S(1)}, bf16[48,64,137]{2,1,0:T(8,128)(2,1)}, u32[]{:S(2)}) copy-start(bf16[48,64,137]{2,1,0:T(8,128)(2,1)} %param.9) | copy-start | bytes 2525188
  9.5 29.1 %copy-start.1 = (s32[32]{0:T(128)S(1)}, s32[32]{0:T(128)}, u32[]{:S(2)}) copy-start(s32[32]{0:T(128)} %param.12) | copy-start | bytes 388
  9.5 30.3 %copy-start.4 = (s32[16]{0:T(128)S(1)}, s32[16]{0:T(128)}, u32[]{:S(2)}) copy-start(s32[16]{0:T(128)} %param.13) | copy-start | bytes 196
  9.5 31.6 %copy-start.2 = (s32[1536]{0:T(1024)S(1)}, s32[1536]{0:T(1024)}, u32[]{:S(2)}) copy-start(s32[1536]{0:T(1024)} %param.11) | copy-start | bytes 18436
  9.5 31.7 %copy-start.3 = (s32[64]{0:T(128)S(1)}, s32[64]{0:T(128)}, u32[]{:S(2)}) copy-start(s32[64]{0:T(128)} %constant.148) | copy-start | bytes 772
  31.1 62.8 %all-to-all-start = ((bf16[32,6,16,384]{3,2,1,0:T(8,128)(2,1)}), bf16[32,6,16,384]{3,2,1,0:T(8,128)(2,1)}, u32[]{:S(2)}, u32[]{:S(2)}) async-start(bf16[32,6,16,384]{3,2,1,0:T(8,128)(2,1)} %copy.19), calls=%async_computation | async-start | bytes 4718592 | tf_op jit(solution)/shard_map/all_to_all | solution.py:302
  94.0 109.5 %slice-start = ((s8[6291456]{0:T(1024)(128)(4,1)}), s8[4194304]{0:T(1024)(128)(4,1)S(1)}, s32[]{:S(2)}) async-start(s8[6291456]{0:T(1024)(128)(4,1)} %bitcast.32), calls=%async_computation.1 | async-start | bytes 8388608
  94.0 109.5 %slice-start.2 = ((s8[6291456]{0:T(1024)(128)(4,1)}), s8[4194304]{0:T(1024)(128)(4,1)S(1)}, s32[]{:S(2)}) async-start(s8[6291456]{0:T(1024)(128)(4,1)} %bitcast.34), calls=%async_computation.3 | async-start | bytes 8388608
  94.0 109.5 %slice-start.1 = ((s8[6291456]{0:T(1024)(128)(4,1)}), s8[2097152]{0:T(1024)(128)(4,1)S(1)}, s32[]{:S(2)}) async-start(s8[6291456]{0:T(1024)(128)(4,1)} %bitcast.32), calls=%async_computation.2 | async-start | bytes 4194304
  94.0 109.5 %slice-start.3 = ((s8[6291456]{0:T(1024)(128)(4,1)}), s8[2097152]{0:T(1024)(128)(4,1)S(1)}, s32[]{:S(2)}) async-start(s8[6291456]{0:T(1024)(128)(4,1)} %bitcast.34), calls=%async_computation.4 | async-start | bytes 4194304

commit v3 on v2

--- a/solution.py
+++ b/solution.py
@@ -97,6 +97,49 @@
 
 GROUP = 8
 BLOCK = 128
+LANES = 128
+
+
+def spread_kernel(legendre_ref, out_ref, place):
+    row_groups, group, half, totals = legendre_ref.shape
+    wide = out_ref.shape[3]
+    depth = group * LANES
+    source = lax.broadcasted_iota(jnp.int32, (depth, depth), 0)
+    target = lax.broadcasted_iota(jnp.int32, (depth, depth), 1)
+    wanted = (source % LANES) * group + source // LANES
+    place[...] = jnp.where(wanted == target, 1.0, 0.0).astype(jnp.bfloat16)
+    for c in range(totals // LANES):
+        rows = [
+            legendre_ref[:, g, :, c * LANES : (c + 1) * LANES].reshape(row_groups * half, LANES)
+            for g in range(group)
+        ]
+        left = jnp.concatenate(rows, axis=1)
+        moved = jnp.dot(left, place[...], preferred_element_type=jnp.float32).astype(jnp.bfloat16)
+        for q in range(group):
+            lane = (c * group + q) * LANES
+            piece = moved[:, q * LANES : (q + 1) * LANES].reshape(row_groups, half, LANES)
+            out_ref[lane // wide, :, :, lane % wide : lane % wide + LANES] = piece
+
+
+def spread(legendre, device_count):
+    own_rows, half, totals = legendre.shape
+    wide = totals // device_count * GROUP
+    depth = GROUP * LANES
+    return pl.pallas_call(
+        spread_kernel,
+        out_shape=jax.ShapeDtypeStruct(
+            (device_count, own_rows // GROUP, half, wide), jnp.bfloat16
+        ),
+        in_specs=[pl.BlockSpec(memory_space=pltpu.VMEM)],
+        out_specs=pl.BlockSpec(memory_space=pltpu.VMEM),
+        scratch_shapes=[pltpu.VMEM((depth, depth), jnp.bfloat16)],
+        compiler_params=pltpu.CompilerParams(vmem_limit_bytes=32 * 1024 * 1024),
+        cost_estimate=pl.CostEstimate(
+            flops=2 * own_rows * half * totals * depth,
+            bytes_accessed=4 * own_rows * half * totals,
+            transcendentals=0,
+        ),
+    )(legendre.reshape(own_rows // GROUP, GROUP, half, totals))
 
 
 def fused_kernel(
@@ -159,35 +202,38 @@
             turned[:, pl.ds(start, GROUP), :] = flipped.reshape(groups, GROUP, pairs)
             return carry
 
-        lax.fori_loop(0, totals, turn, 0, unroll=4)
+        lax.fori_loop(0, totals, turn, 0, unroll=8)
         same = lax.broadcasted_iota(jnp.int32, (GROUP, depth), 1) % GROUP == lax.broadcasted_iota(
             jnp.int32, (GROUP, depth), 0
         )
         pick = pick_ref[step % 2]
 
-        def group_sum(g, slot):
+        def choose(g, carry):
             table = table_ref[g].astype(jnp.float32)
             masks = mask_ref[g]
             both = jnp.concatenate([table * masks[0:1, :], table * masks[1:2, :]], axis=0)
-            picked[slot] = jnp.dot(
+            picked[g] = jnp.dot(
                 pick, both.astype(jnp.bfloat16), preferred_element_type=jnp.float32
             )
-            rows = []
-            for t in range(lats):
-                rows.append(jnp.where(same, picked[slot, t : t + 1, :], 0.0))
+            return carry
+
+        lax.fori_loop(0, groups, choose, 0, unroll=8)
+
+        def group_sum(g):
+            rows = [jnp.where(same, picked[g, t : t + 1, :], 0.0) for t in range(lats)]
             left = jnp.concatenate(rows, axis=0).astype(jnp.bfloat16)
             right = turned[g].astype(jnp.bfloat16)
             total = jnp.dot(left, right, preferred_element_type=jnp.float32)
             return total.reshape(lats, GROUP, pairs)
 
         def pair_of_groups(h, carry):
-            both = jnp.concatenate([group_sum(2 * h, 0), group_sum(2 * h + 1, 1)], axis=1)
+            both = jnp.concatenate([group_sum(2 * h), group_sum(2 * h + 1)], axis=1)
             both = both.astype(jnp.bfloat16).reshape(2, 2, 2, z_count, 2 * GROUP, pairs)
             start = pl.multiple_of(h * 2 * GROUP, 2 * GROUP)
             part[step, :, :, :, :, pl.ds(start, 2 * GROUP), :] = both
             return carry
 
-        lax.fori_loop(0, groups // 2, pair_of_groups, 0)
+        lax.fori_loop(0, groups // 2, pair_of_groups, 0, unroll=2)
         hop(step, 0).start()
 
     def add(to, arrived):
@@ -265,7 +311,7 @@
         out_specs=pl.BlockSpec((rows, pairs), lambda b: (0, 0)),
         scratch_shapes=[
             pltpu.VMEM((groups, depth, pairs), jnp.float32),
-            pltpu.VMEM((2, lats, depth), jnp.float32),
+            pltpu.VMEM((groups, lats, depth), jnp.float32),
             pltpu.VMEM((blocks, 2, 2, 2, z_count) + tile, jnp.bfloat16),
             pltpu.VMEM((blocks, 2, 2, z_count) + tile, jnp.bfloat16),
             pltpu.VMEM((blocks, 2, z_count) + tile, jnp.bfloat16),
@@ -295,10 +341,7 @@
     flat_index = lax.axis_index(("wave", "lev"))
     total_ids = flat_index * own_totals + jnp.arange(own_totals, dtype=jnp.int32)
 
-    table = legendre.reshape(own_rows // GROUP, GROUP, device_count, own_totals, half_lats)
-    table = jnp.transpose(table, (2, 0, 4, 3, 1)).reshape(
-        device_count, own_rows // GROUP, half_lats, own_totals * GROUP
-    )
+    table = spread(jnp.transpose(legendre, (0, 2, 1)), device_count)
     table = lax.all_to_all(table, ("wave", "lev"), split_axis=0, concat_axis=0, tiled=True)
     table = table.reshape(total // GROUP, half_lats, own_totals * GROUP)
 
@@ -342,6 +385,7 @@
     devices = lax.axis_size("wave") * lax.axis_size("lev")
     smaller = 2 * legendre.shape[2] < own_totals
     fits = total % BLOCK == 0 and legendre.shape[0] % GROUP == 0 and lat_order.shape[0] == devices
+    fits = fits and total % LANES == 0 and total // devices * GROUP % LANES == 0
     fits = fits and lax.axis_size("lev") == 2 and lax.axis_size("wave") % 4 == 0
     if smaller and fits:
         return reduce_partials(*arrays)

time: 209 us -> 164 us (0.78)
  local copies, waits for them, and re-layouts: 33.8 us -> 5.86 us
  Pallas kernels: 109 us -> 92.4 us
    reshape x3 -> x0, local copies, waits for them, and re-layouts: 31.1 us -> none  [the longest x2 21.4 us: reduce_partials(): legendre.reshape(own_rows // GROUP, GROUP, device_count, own_totals, half...]
    pallas_call x1, Pallas kernels: 109 us -> 88 us  [reduced_sums(): pl.pallas_call(fused_kernel, grid=(blocks + 4,), in_specs=[pl.BlockSpec((...]
    pallas_call x0 -> x1, Pallas kernels: none -> 4.41 us  [spread(): pl.pallas_call(spread_kernel, out_shape=jax.ShapeDtypeStruct((device_coun...]
    unnamed x18 -> x24, local copies, waits for them, and re-layouts: 0.04 us -> 3.26 us
  transfers between devices with their start and end apart: 1 -> 1, of which waited for: 0 -> 0; matrix products, arithmetic and copies ran while one was open for 26% -> 33% of each run, Pallas kernels for 0% -> 0%
where the time goes in v3:
time: 164 us
  Pallas kernels  92.4 us (56%)
  other arithmetic  28.9 us (18%)
  matrix products  27.5 us (17%)
  starting transfers between devices  7.59 us (5%)
  local copies, waits for them, and re-layouts  5.86 us (4%)
    pallas_call x1, Pallas kernels, reduced_sums(): pl.pallas_call(fused_kernel, grid=(blocks + 4,), in_specs=[pl.BlockSpec((...  88 us
    dot_general x1, matrix products, reduce_partials(): jnp.einsum('nrcl,nsl->ncsr', control, covariance, preferred_element_type=...  22.8 us
    convert_element_type x1, other arithmetic, trig_tables(): sin_part = (-factor[:, None] * sine).astype(jnp.bfloat16)  11.9 us
    all_to_all x1, starting transfers between devices, reduce_partials(): lax.all_to_all(table, ('wave', 'lev'), split_axis=0, concat_axis=0, tiled...  7.59 us
    sub x1, other arithmetic, trig_tables(): cosine = (cos_c * cos_f - sin_c * sin_f).reshape(orders.shape[0], width)  6.88 us
    cos x1, other arithmetic, trig_tables(): cos_f = jnp.cos(fine_angle)[:, None, :]  5.18 us
    dot_general x1, matrix products, fourier(): jnp.einsum('ks,kj->sj', stacked, trig_table, preferred_element_type=jnp.f...  4.68 us
    pallas_call x1, Pallas kernels, spread(): pl.pallas_call(spread_kernel, out_shape=jax.ShapeDtypeStruct((device_coun...  4.41 us
  transfers between devices with their start and end apart: 1, of which 0 were waited for; matrix products, arithmetic and copies ran while one was open for 33% of the time, Pallas kernels for 0%

profile of v3, /device:TPU:0, one launch (start us, length us, event | category | flops | bytes accessed | tf_op | source)
XLA Modules:
  0.0 163.9 jit_solution(5983309043967487757)
XLA Ops:
  0.0 0.0 copy-start
  0.0 0.0 copy-start.6
  0.0 0.0 copy-start.4
  0.0 0.0 copy-start.7
  0.0 0.0 copy-start.3
  0.0 1.8 %copy-done.3 = bf16[48,1536,16]{1,2,0:T(8,128)(2,1)S(1)} copy-done((bf16[48,1536,16]{1,2,0:T(8,128)(2,1)S(1)}, bf16[48,1536,16]{1,2,0:T(8,128)(2,1)}, u32[]{:S(2)}) %copy-start.3) | copy-done | bytes 2359320
  1.8 0.0 copy-start.5
  1.8 4.4 %shard_map.82 = bf16[32,6,16,384]{3,2,1,0:T(8,128)(2,1)S(1)} custom-call(bf16[6,8,16,1536]{3,2,1,0:T(8,128)(2,1)S(1)} %bitcast.28), custom_call_target="tpu_custom_call" | custom-call | flops 2415919104 | bytes 4718592 | tf_op jit(solution)/shard_map/pallas_call | solution.py:128
  6.2 0.0 copy-start.2
  6.3 1.4 copy-done.2
  7.7 7.6 %all-to-all-start = ((bf16[32,6,16,384]{3,2,1,0:T(8,128)(2,1)}), bf16[32,6,16,384]{3,2,1,0:T(8,128)(2,1)}, u32[]{:S(2)}, u32[]{:S(2)}) async-start(bf16[32,6,16,384]{3,2,1,0:T(8,128)(2,1)} %copy-done.2), calls=%async_computation | async-start | bytes 4718592 | tf_op jit(solution)/shard_map/all_to_all | solution.py:345
  15.3 0.0 copy-done.4
  15.3 0.6 dynamic-slice.4
  16.5 0.0 copy-done.7
  16.5 0.6 dynamic-slice.5
  17.8 0.0 copy-done.5
  17.8 0.1 ge.45
  18.0 5.2 %fusion.26 = (f32[1536,64]{0,1:T(8,128)S(1)}, f32[1536,64]{0,1:T(8,128)S(1)}) fusion(f32[]{:T(128)S(6)} %div.3, s32[]{:T(128)S(6)} %select_n.123, s32[1536]{0:T(1024)S(1)} %copy-done.5, pred[]{:T(512)S(6)} %lt.53), kind=kLoop, calls=%fused_computation.34 | loop fusion | flops 983040 | bytes 792585 | tf_op jit(solution)/shard_map/cos | solution.py:20
  23.1 2.7 %fusion.35 = (f32[1536,32]{0,1:T(8,128)S(1)}, f32[1536,32]{0,1:T(8,128)S(1)}) fusion(f32[]{:T(128)S(6)} %div.3, s32[]{:T(128)S(6)} %select_n.123, s32[32]{0:T(128)S(1)} %iota_multiply_fusion, s32[1536]{0:T(1024)S(1)} %copy-done.5, pred[]{:T(512)S(6)} %lt.53), kind=kLoop, calls=%fused_computation.46 | loop fusion | flops 491520 | bytes 399497 | tf_op jit(solution)/shard_map/cos | solution.py:18
  25.9 0.1 ge.42
  25.9 0.1 ge.43
  26.0 0.1 copy.11
  26.1 0.2 copy.12
  26.3 0.0 copy-done.6
  26.4 0.8 gather_fusion
  27.1 0.1 reshape.351
  27.2 0.1 fusion.38.pick_ref
  27.3 1.3 compare_select_fusion.4
  28.6 0.5 pad_maximum_fusion.mask_ref
  29.1 6.9 %multiply_subtract_fusion = (f32[1536,32,64]{0,2,1:T(8,128)S(1)}, f32[1536,32,64]{0,2,1:T(8,128)}) fusion(f32[1536,64]{0,1:T(8,128)S(1)} %get-tuple-element.38, f32[1536,32]{0,1:T(8,128)S(1)} %get-tuple-element.34, f32[1536,64]{0,1:T(8,128)S(1)} %get-tuple-element.37, f32[1536,32]{0,1:T(8,128)S(1)} %get-tuple-element.33), kind=kLoop, calls=%fused_computation.13 | loop fusion | flops 18874368 | bytes 26345472 | tf_op jit(solution)/shard_map/sub | solution.py:22
  36.0 11.9 %fusion.9 = (bf16[1536,2048]{0,1:T(8,128)(2,1)}, bf16[1536,2048]{0,1:T(8,128)(2,1)}) fusion(f32[1536,32,64]{0,2,1:T(8,128)} %get-tuple-element.28, f32[1536]{0:T(1024)S(1)} %get-tuple-element.36, f32[1536,32,64]{0,2,1:T(8,128)S(1)} %get-tuple-element.27, f32[1536]{0:T(1024)S(1)} %get-tuple-element.35), kind=kLoop, calls=%fused_computation.9 | loop fusion | flops 12582912 | bytes 37761024 | tf_op jit(solution)/shard_map/convert_element_type | solution.py:25
  47.9 0.0 copy-done
  47.9 22.8 %fusion.2 = bf16[48,64,1536,2]{2,1,3,0:T(8,128)(2,1)} fusion(bf16[48,1536,2,137]{1,2,3,0:T(2,128)(2,1)} %param.8, bf16[48,64,137]{2,1,0:T(8,128)(2,1)S(1)} %copy-done), kind=kOutput, calls=%fused_computation.3 | convolution fusion | flops 2595225600 | bytes 60119040 | tf_op jit(solution)/shard_map/nrcl,nsl->ncsr/dot_general | solution.py:354
  70.7 0.0 all-to-all-done
  70.7 0.0 slice-start
  70.7 0.0 slice-start.2
  70.7 0.0 slice-start.1
  70.7 0.0 slice-start.3
  70.7 0.0 copy-start.1
  70.8 88.0 %shard_map.83 = bf16[1536,128]{1,0:T(8,128)(2,1)S(1)} custom-call(bf16[2,32,32]{2,1,0:T(8,128)(2,1)S(1)} %fusion.38.pick_ref, bf16[48,128,1536]{2,1,0:T(8,128)(2,1)} %bitcast.29, bf16[192,16,384]{2,1,0:T(8,128)(2,1)} %bitcast.6.table_ref, f32[192,2,384]{2,1,0:T(2,128)S(1)} %pad_maximum_fusion.mask_ref), custom_call_target="tpu_custom_call" | custom-call | flops 4831838208 | bytes 18874368 | tf_op jit(solution)/shard_map/pallas_call | solution.py:302
  158.8 0.4 fusion.41
  159.2 0.0 slice-done
  159.2 0.0 slice-done.2
  159.2 0.0 slice-done.1
  159.2 0.0 slice-done.3
  159.2 4.7 %fusion.14 = bf16[1,64,2048]{2,1,0:T(8,128)(2,1)} fusion(bf16[1536,2048]{0,1:T(8,128)(2,1)S(1)} %bitcast.31, bf16[1536,2048]{0,1:T(8,128)(2,1)S(1)} %bitcast.33, bf16[1536,64]{1,0:T(8,128)(2,1)S(1)} %get-tuple-element.30, bf16[1536,64]{1,0:T(8,128)(2,1)S(1)} %get-tuple-element.29), kind=kOutput, calls=%fused_computation.15 | convolution fusion | flops 831389696 | bytes 13238272 | tf_op jit(solution)/shard_map/ks,kj->sj/dot_general | solution.py:378
  163.9 0.0 copy-done.1
  (8 shorter events, 0.1 us)
Async XLA Ops:
  0.0 47.9 %copy-start = (bf16[48,64,137]{2,1,0:T(8,128)(2,1)S(1)}, bf16[48,64,137]{2,1,0:T(8,128)(2,1)}, u32[]{:S(2)}) copy-start(bf16[48,64,137]{2,1,0:T(8,128)(2,1)} %param.9) | copy-start | bytes 2525188
  0.0 26.3 %copy-start.6 = (s32[64]{0:T(128)S(1)}, s32[64]{0:T(128)}, u32[]{:S(2)}) copy-start(s32[64]{0:T(128)} %constant.148) | copy-start | bytes 772
  0.0 15.3 %copy-start.4 = (s32[32]{0:T(128)S(1)}, s32[32]{0:T(128)}, u32[]{:S(2)}) copy-start(s32[32]{0:T(128)} %param.12) | copy-start | bytes 388
  0.0 16.5 %copy-start.7 = (s32[16]{0:T(128)S(1)}, s32[16]{0:T(128)}, u32[]{:S(2)}) copy-start(s32[16]{0:T(128)} %param.13) | copy-start | bytes 196
  0.0 1.8 %copy-start.3 = (bf16[48,1536,16]{1,2,0:T(8,128)(2,1)S(1)}, bf16[48,1536,16]{1,2,0:T(8,128)(2,1)}, u32[]{:S(2)}) copy-start(bf16[48,1536,16]{1,2,0:T(8,128)(2,1)} %param.10) | copy-start | bytes 7077892
  1.8 15.9 %copy-start.5 = (s32[1536]{0:T(1024)S(1)}, s32[1536]{0:T(1024)}, u32[]{:S(2)}) copy-start(s32[1536]{0:T(1024)} %param.11) | copy-start | bytes 18436
  6.2 1.4 copy-start.2
  7.7 63.1 %all-to-all-start = ((bf16[32,6,16,384]{3,2,1,0:T(8,128)(2,1)}), bf16[32,6,16,384]{3,2,1,0:T(8,128)(2,1)}, u32[]{:S(2)}, u32[]{:S(2)}) async-start(bf16[32,6,16,384]{3,2,1,0:T(8,128)(2,1)} %copy-done.2), calls=%async_computation | async-start | bytes 4718592 | tf_op jit(solution)/shard_map/all_to_all | solution.py:345
  70.7 88.5 %slice-start = ((s8[6291456]{0:T(1024)(128)(4,1)}), s8[4194304]{0:T(1024)(128)(4,1)S(1)}, s32[]{:S(2)}) async-start(s8[6291456]{0:T(1024)(128)(4,1)} %bitcast.30), calls=%async_computation.1 | async-start | bytes 8388608
  70.7 88.5 %slice-start.2 = ((s8[6291456]{0:T(1024)(128)(4,1)}), s8[4194304]{0:T(1024)(128)(4,1)S(1)}, s32[]{:S(2)}) async-start(s8[6291456]{0:T(1024)(128)(4,1)} %bitcast.32), calls=%async_computation.3 | async-start | bytes 8388608
  70.7 88.5 %slice-start.1 = ((s8[6291456]{0:T(1024)(128)(4,1)}), s8[2097152]{0:T(1024)(128)(4,1)S(1)}, s32[]{:S(2)}) async-start(s8[6291456]{0:T(1024)(128)(4,1)} %bitcast.30), calls=%async_computation.2 | async-start | bytes 4194304
  70.7 88.5 %slice-start.3 = ((s8[6291456]{0:T(1024)(128)(4,1)}), s8[2097152]{0:T(1024)(128)(4,1)S(1)}, s32[]{:S(2)}) async-start(s8[6291456]{0:T(1024)(128)(4,1)} %bitcast.32), calls=%async_computation.4 | async-start | bytes 4194304
  70.7 93.2 %copy-start.1 = (bf16[48,64,137]{2,1,0:T(8,128)(2,1)S(1)}, bf16[48,64,137]{2,1,0:T(8,128)(2,1)}, u32[]{:S(2)}) copy-start(bf16[48,64,137]{2,1,0:T(8,128)(2,1)} %param.9) | copy-start | bytes 2525188

commit v4 on v3

--- a/solution.py
+++ b/solution.py
@@ -202,7 +202,7 @@
             turned[:, pl.ds(start, GROUP), :] = flipped.reshape(groups, GROUP, pairs)
             return carry
 
-        lax.fori_loop(0, totals, turn, 0, unroll=8)
+        lax.fori_loop(0, totals, turn, 0, unroll=16)
         same = lax.broadcasted_iota(jnp.int32, (GROUP, depth), 1) % GROUP == lax.broadcasted_iota(
             jnp.int32, (GROUP, depth), 0
         )
@@ -217,7 +217,7 @@
             )
             return carry
 
-        lax.fori_loop(0, groups, choose, 0, unroll=8)
+        lax.fori_loop(0, groups, choose, 0, unroll=16)
 
         def group_sum(g):
             rows = [jnp.where(same, picked[g, t : t + 1, :], 0.0) for t in range(lats)]
@@ -233,7 +233,7 @@
             part[step, :, :, :, :, pl.ds(start, 2 * GROUP), :] = both
             return carry
 
-        lax.fori_loop(0, groups // 2, pair_of_groups, 0, unroll=2)
+        lax.fori_loop(0, groups // 2, pair_of_groups, 0, unroll=4)
         hop(step, 0).start()
 
     def add(to, arrived):

time: 164 us -> 160 us (0.976)
  Pallas kernels: 92.4 us -> 87.7 us
    pallas_call x1, Pallas kernels: 88 us -> 83.3 us  [reduced_sums(): pl.pallas_call(fused_kernel, grid=(blocks + 4,), in_specs=[pl.BlockSpec((...]
  transfers between devices with their start and end apart: 1 -> 1, of which waited for: 0 -> 0; matrix products, arithmetic and copies ran while one was open for 33% -> 34% of each run, Pallas kernels for 0% -> 0%
where the time goes in v4:
time: 160 us; the launch traced here: 159 us
  Pallas kernels  87.7 us (55%)
  other arithmetic  28.9 us (18%)
  matrix products  27.5 us (17%)
  starting transfers between devices  7.59 us (5%)
  local copies, waits for them, and re-layouts  5.86 us (4%)
    pallas_call x1, Pallas kernels, reduced_sums(): pl.pallas_call(fused_kernel, grid=(blocks + 4,), in_specs=[pl.BlockSpec((...  83.3 us
    dot_general x1, matrix products, reduce_partials(): jnp.einsum('nrcl,nsl->ncsr', control, covariance, preferred_element_type=...  22.8 us
    convert_element_type x1, other arithmetic, trig_tables(): sin_part = (-factor[:, None] * sine).astype(jnp.bfloat16)  11.9 us
    all_to_all x1, starting transfers between devices, reduce_partials(): lax.all_to_all(table, ('wave', 'lev'), split_axis=0, concat_axis=0, tiled...  7.59 us
    sub x1, other arithmetic, trig_tables(): cosine = (cos_c * cos_f - sin_c * sin_f).reshape(orders.shape[0], width)  6.88 us
    cos x1, other arithmetic, trig_tables(): cos_f = jnp.cos(fine_angle)[:, None, :]  5.18 us
    dot_general x1, matrix products, fourier(): jnp.einsum('ks,kj->sj', stacked, trig_table, preferred_element_type=jnp.f...  4.69 us
    pallas_call x1, Pallas kernels, spread(): pl.pallas_call(spread_kernel, out_shape=jax.ShapeDtypeStruct((device_coun...  4.41 us
  transfers between devices with their start and end apart: 1, of which 0 were waited for; matrix products, arithmetic and copies ran while one was open for 34% of the time, Pallas kernels for 0%

profile of v4, /device:TPU:0, one launch (start us, length us, event | category | flops | bytes accessed | tf_op | source)
XLA Modules:
  0.0 159.2 jit_solution(12308853416409351801)
XLA Ops:
  0.0 0.0 copy-start
  0.0 0.0 copy-start.6
  0.0 0.0 copy-start.4
  0.0 0.0 copy-start.7
  0.0 0.0 copy-start.3
  0.0 1.8 %copy-done.3 = bf16[48,1536,16]{1,2,0:T(8,128)(2,1)S(1)} copy-done((bf16[48,1536,16]{1,2,0:T(8,128)(2,1)S(1)}, bf16[48,1536,16]{1,2,0:T(8,128)(2,1)}, u32[]{:S(2)}) %copy-start.3) | copy-done | bytes 2359320
  1.8 0.0 copy-start.5
  1.8 4.4 %shard_map.82 = bf16[32,6,16,384]{3,2,1,0:T(8,128)(2,1)S(1)} custom-call(bf16[6,8,16,1536]{3,2,1,0:T(8,128)(2,1)S(1)} %bitcast.28), custom_call_target="tpu_custom_call" | custom-call | flops 2415919104 | bytes 4718592 | tf_op jit(solution)/shard_map/pallas_call | solution.py:128
  6.2 0.0 copy-start.2
  6.3 1.4 copy-done.2
  7.7 7.6 %all-to-all-start = ((bf16[32,6,16,384]{3,2,1,0:T(8,128)(2,1)}), bf16[32,6,16,384]{3,2,1,0:T(8,128)(2,1)}, u32[]{:S(2)}, u32[]{:S(2)}) async-start(bf16[32,6,16,384]{3,2,1,0:T(8,128)(2,1)} %copy-done.2), calls=%async_computation | async-start | bytes 4718592 | tf_op jit(solution)/shard_map/all_to_all | solution.py:345
  15.3 0.0 copy-done.4
  15.3 0.6 dynamic-slice.4
  16.5 0.0 copy-done.7
  16.5 0.6 dynamic-slice.5
  17.8 0.0 copy-done.5
  17.8 0.1 ge.45
  18.0 5.2 %fusion.26 = (f32[1536,64]{0,1:T(8,128)S(1)}, f32[1536,64]{0,1:T(8,128)S(1)}) fusion(f32[]{:T(128)S(6)} %div.3, s32[]{:T(128)S(6)} %select_n.123, s32[1536]{0:T(1024)S(1)} %copy-done.5, pred[]{:T(512)S(6)} %lt.53), kind=kLoop, calls=%fused_computation.34 | loop fusion | flops 983040 | bytes 792585 | tf_op jit(solution)/shard_map/cos | solution.py:20
  23.1 2.7 %fusion.35 = (f32[1536,32]{0,1:T(8,128)S(1)}, f32[1536,32]{0,1:T(8,128)S(1)}) fusion(f32[]{:T(128)S(6)} %div.3, s32[]{:T(128)S(6)} %select_n.123, s32[32]{0:T(128)S(1)} %iota_multiply_fusion, s32[1536]{0:T(1024)S(1)} %copy-done.5, pred[]{:T(512)S(6)} %lt.53), kind=kLoop, calls=%fused_computation.46 | loop fusion | flops 491520 | bytes 399497 | tf_op jit(solution)/shard_map/cos | solution.py:18
  25.9 0.1 ge.42
  25.9 0.1 ge.43
  26.0 0.1 copy.11
  26.1 0.2 copy.12
  26.3 0.0 copy-done.6
  26.4 0.8 gather_fusion
  27.1 0.1 reshape.351
  27.2 0.1 fusion.38.pick_ref
  27.3 1.3 compare_select_fusion.4
  28.6 0.5 pad_maximum_fusion.mask_ref
  29.1 6.9 %multiply_subtract_fusion = (f32[1536,32,64]{0,2,1:T(8,128)S(1)}, f32[1536,32,64]{0,2,1:T(8,128)}) fusion(f32[1536,64]{0,1:T(8,128)S(1)} %get-tuple-element.38, f32[1536,32]{0,1:T(8,128)S(1)} %get-tuple-element.34, f32[1536,64]{0,1:T(8,128)S(1)} %get-tuple-element.37, f32[1536,32]{0,1:T(8,128)S(1)} %get-tuple-element.33), kind=kLoop, calls=%fused_computation.13 | loop fusion | flops 18874368 | bytes 26345472 | tf_op jit(solution)/shard_map/sub | solution.py:22
  36.0 11.9 %fusion.9 = (bf16[1536,2048]{0,1:T(8,128)(2,1)}, bf16[1536,2048]{0,1:T(8,128)(2,1)}) fusion(f32[1536,32,64]{0,2,1:T(8,128)} %get-tuple-element.28, f32[1536]{0:T(1024)S(1)} %get-tuple-element.36, f32[1536,32,64]{0,2,1:T(8,128)S(1)} %get-tuple-element.27, f32[1536]{0:T(1024)S(1)} %get-tuple-element.35), kind=kLoop, calls=%fused_computation.9 | loop fusion | flops 12582912 | bytes 37761024 | tf_op jit(solution)/shard_map/convert_element_type | solution.py:25
  47.9 0.0 copy-done
  47.9 22.8 %fusion.2 = bf16[48,64,1536,2]{2,1,3,0:T(8,128)(2,1)} fusion(bf16[48,1536,2,137]{1,2,3,0:T(2,128)(2,1)} %param.8, bf16[48,64,137]{2,1,0:T(8,128)(2,1)S(1)} %copy-done), kind=kOutput, calls=%fused_computation.3 | convolution fusion | flops 2595225600 | bytes 60119040 | tf_op jit(solution)/shard_map/nrcl,nsl->ncsr/dot_general | solution.py:354
  70.7 0.0 all-to-all-done
  70.7 0.0 slice-start
  70.7 0.0 slice-start.2
  70.7 0.0 slice-start.1
  70.7 0.0 slice-start.3
  70.7 0.0 copy-start.1
  70.8 83.3 %shard_map.83 = bf16[1536,128]{1,0:T(8,128)(2,1)S(1)} custom-call(bf16[2,32,32]{2,1,0:T(8,128)(2,1)S(1)} %fusion.38.pick_ref, bf16[48,128,1536]{2,1,0:T(8,128)(2,1)} %bitcast.29, bf16[192,16,384]{2,1,0:T(8,128)(2,1)} %bitcast.6.table_ref, f32[192,2,384]{2,1,0:T(2,128)S(1)} %pad_maximum_fusion.mask_ref), custom_call_target="tpu_custom_call" | custom-call | flops 4831838208 | bytes 18874368 | tf_op jit(solution)/shard_map/pallas_call | solution.py:302
  154.1 0.4 fusion.41
  154.5 0.0 slice-done
  154.5 0.0 slice-done.2
  154.5 0.0 slice-done.1
  154.5 0.0 slice-done.3
  154.5 4.7 %fusion.14 = bf16[1,64,2048]{2,1,0:T(8,128)(2,1)} fusion(bf16[1536,2048]{0,1:T(8,128)(2,1)S(1)} %bitcast.31, bf16[1536,2048]{0,1:T(8,128)(2,1)S(1)} %bitcast.33, bf16[1536,64]{1,0:T(8,128)(2,1)S(1)} %get-tuple-element.30, bf16[1536,64]{1,0:T(8,128)(2,1)S(1)} %get-tuple-element.29), kind=kOutput, calls=%fused_computation.15 | convolution fusion | flops 831389696 | bytes 13238272 | tf_op jit(solution)/shard_map/ks,kj->sj/dot_general | solution.py:378
  159.2 0.0 copy-done.1
  (8 shorter events, 0.1 us)
Async XLA Ops:
  0.0 47.9 %copy-start = (bf16[48,64,137]{2,1,0:T(8,128)(2,1)S(1)}, bf16[48,64,137]{2,1,0:T(8,128)(2,1)}, u32[]{:S(2)}) copy-start(bf16[48,64,137]{2,1,0:T(8,128)(2,1)} %param.9) | copy-start | bytes 2525188
  0.0 26.3 %copy-start.6 = (s32[64]{0:T(128)S(1)}, s32[64]{0:T(128)}, u32[]{:S(2)}) copy-start(s32[64]{0:T(128)} %constant.148) | copy-start | bytes 772
  0.0 15.3 %copy-start.4 = (s32[32]{0:T(128)S(1)}, s32[32]{0:T(128)}, u32[]{:S(2)}) copy-start(s32[32]{0:T(128)} %param.12) | copy-start | bytes 388
  0.0 16.5 %copy-start.7 = (s32[16]{0:T(128)S(1)}, s32[16]{0:T(128)}, u32[]{:S(2)}) copy-start(s32[16]{0:T(128)} %param.13) | copy-start | bytes 196
  0.0 1.8 %copy-start.3 = (bf16[48,1536,16]{1,2,0:T(8,128)(2,1)S(1)}, bf16[48,1536,16]{1,2,0:T(8,128)(2,1)}, u32[]{:S(2)}) copy-start(bf16[48,1536,16]{1,2,0:T(8,128)(2,1)} %param.10) | copy-start | bytes 7077892
  1.8 15.9 %copy-start.5 = (s32[1536]{0:T(1024)S(1)}, s32[1536]{0:T(1024)}, u32[]{:S(2)}) copy-start(s32[1536]{0:T(1024)} %param.11) | copy-start | bytes 18436
  6.2 1.4 copy-start.2
  7.7 63.1 %all-to-all-start = ((bf16[32,6,16,384]{3,2,1,0:T(8,128)(2,1)}), bf16[32,6,16,384]{3,2,1,0:T(8,128)(2,1)}, u32[]{:S(2)}, u32[]{:S(2)}) async-start(bf16[32,6,16,384]{3,2,1,0:T(8,128)(2,1)} %copy-done.2), calls=%async_computation | async-start | bytes 4718592 | tf_op jit(solution)/shard_map/all_to_all | solution.py:345
  70.7 83.8 %slice-start = ((s8[6291456]{0:T(1024)(128)(4,1)}), s8[4194304]{0:T(1024)(128)(4,1)S(1)}, s32[]{:S(2)}) async-start(s8[6291456]{0:T(1024)(128)(4,1)} %bitcast.30), calls=%async_computation.1 | async-start | bytes 8388608
  70.7 83.8 %slice-start.2 = ((s8[6291456]{0:T(1024)(128)(4,1)}), s8[4194304]{0:T(1024)(128)(4,1)S(1)}, s32[]{:S(2)}) async-start(s8[6291456]{0:T(1024)(128)(4,1)} %bitcast.32), calls=%async_computation.3 | async-start | bytes 8388608
  70.7 83.8 %slice-start.1 = ((s8[6291456]{0:T(1024)(128)(4,1)}), s8[2097152]{0:T(1024)(128)(4,1)S(1)}, s32[]{:S(2)}) async-start(s8[6291456]{0:T(1024)(128)(4,1)} %bitcast.30), calls=%async_computation.2 | async-start | bytes 4194304
  70.7 83.8 %slice-start.3 = ((s8[6291456]{0:T(1024)(128)(4,1)}), s8[2097152]{0:T(1024)(128)(4,1)S(1)}, s32[]{:S(2)}) async-start(s8[6291456]{0:T(1024)(128)(4,1)} %bitcast.32), calls=%async_computation.4 | async-start | bytes 4194304
  70.7 88.5 %copy-start.1 = (bf16[48,64,137]{2,1,0:T(8,128)(2,1)S(1)}, bf16[48,64,137]{2,1,0:T(8,128)(2,1)}, u32[]{:S(2)}) copy-start(bf16[48,64,137]{2,1,0:T(8,128)(2,1)} %param.9) | copy-start | bytes 2525188
